TPU v7x, 512 devices: a whole 4x8x8 slice. The times are simulated.
512 devices in a mesh: row: 32 (over z_hi, y, core), col: 16 (over z_lo, x).
Axes of the slice: x: 4, y: 8, z: 8 (z_hi: 2, z_lo: 4; z = z_hi * 4 + z_lo), core: 2. Of those that a mesh axis runs over, the one named last changes fastest.
Arguments:
- pair_rep: bfloat16 [1024, 1024, 128], P('row', 'col'), may hold values from -6 to 6
- in_gain: float32 [2, 128], replicated, may hold values from 0.1 to 1.9
- in_bias: float32 [2, 128], replicated, may hold values from -3 to 3
- proj_w: bfloat16 [2, 128, 512], replicated, may hold values from -0.5 to 0.5
- gate_w: bfloat16 [2, 128, 128], replicated, may hold values from -0.5 to 0.5
- out_gain: float32 [2, 128], replicated, may hold values from 0.1 to 1.9
- out_bias: float32 [2, 128], replicated, may hold values from -3 to 3
- out_w: bfloat16 [2, 128, 128], replicated, may hold values from -0.5 to 0.5
Outputs:
- pair_out: bfloat16 [1024, 1024, 128], P('row', 'col')
All inputs are finite; a program needn't handle non-finite values.
Results may differ from a plain program's by a relative error of at most 0.007.
Values may be sent and summed in bfloat16 or wider, within the bound.
No kernel may reach another device: no remote copies, remote signals or barrier semaphores. Data moves between devices by JAX's collectives and lax.ppermute only.
A program may use at most 64 MiB of HBM per device.

v0:
```python
import functools

import jax
import jax.numpy as jnp
from jax import lax
from jax.experimental import pallas as pl
from jax.experimental.pallas import tpu as pltpu
from jax.sharding import Mesh
from jax.sharding import PartitionSpec as P

GROUP = ("zhi", "y", "core", "zlo")
EPS = 1e-05
F32 = jnp.float32
BF16 = jnp.bfloat16


def _params(mib):
    return pltpu.CompilerParams(vmem_limit_bytes=mib << 20)


def _norm(values, axis, gain, bias):
    center = values - jnp.mean(values, axis=axis, keepdims=True)
    spread = jnp.mean(center * center, axis=axis, keepdims=True)
    return center * lax.rsqrt(spread + EPS) * gain + bias


def _project(cells, gain, bias, turned_w, gate_w):
    normed = _norm(cells, 1, gain, bias).astype(BF16)
    halves = lax.dot_general(
        turned_w, normed, (((1,), (1,)), ((), ())), preferred_element_type=F32
    )
    left = jax.nn.sigmoid(halves[128:256]) * halves[:128]
    right = jax.nn.sigmoid(halves[384:]) * halves[256:384]
    gate = jax.nn.sigmoid(jnp.dot(normed, gate_w, preferred_element_type=F32))
    return left, right, gate


def _rows(ref, s):
    return jnp.concatenate([ref[s], ref[16 + s]], axis=0)


def _put_rows(ref, s, value):
    ref[s] = value[:64]
    ref[16 + s] = value[64:]


def _first_kernel(p_ref, gain_ref, bias_ref, w_ref, gw_ref, out_ref, gate_ref, scr):
    turned_w = w_ref[...].T
    for s in range(16):
        cells = _rows(p_ref, s).astype(F32)
        left, right, gate = _project(cells, gain_ref[...], bias_ref[...], turned_w, gw_ref[...])
        scr[pl.ds(s, 128, stride=32), :] = left
        scr[pl.ds(16 + s, 128, stride=32), :] = right
        _put_rows(gate_ref, s, gate)
    out_ref[...] = scr[...].astype(BF16)


def _finished(scr, s, cells, gate, gain, bias, out_w):
    tri = scr[pl.ds(s, 128, stride=16), :]
    mixed = _norm(tri, 0, gain, bias).astype(BF16)
    projected = lax.dot_general(
        mixed, out_w, (((0,), (0,)), ((), ())), preferred_element_type=F32
    )
    return (cells + gate * projected).astype(BF16)


def _middle_kernel(
    t_ref, p_ref, g_ref, og_ref, ob_ref, ow_ref, gain_ref, bias_ref, w_ref, gw_ref,
    mid_ref, left_ref, right_ref, gate_ref, tri_scr, left_scr, right_scr,
):
    tri_scr[...] = t_ref[...].astype(F32)
    turned_w = w_ref[...].T
    for s in range(16):
        cells = _rows(p_ref, s).astype(F32)
        mid = _finished(tri_scr, s, cells, _rows(g_ref, s), og_ref[...], ob_ref[...], ow_ref[...])
        _put_rows(mid_ref, s, mid)
        left, right, gate = _project(
            mid.astype(F32), gain_ref[...], bias_ref[...], turned_w, gw_ref[...]
        )
        left_scr[pl.ds(s, 128, stride=16), :] = left
        right_scr[pl.ds(s, 128, stride=16), :] = right
        _put_rows(gate_ref, s, gate)
    left_ref[...] = left_scr[...].astype(BF16)
    right_ref[...] = right_scr[...].astype(BF16)


def _last_kernel(t_ref, p_ref, g_ref, og_ref, ob_ref, ow_ref, out_ref, tri_scr):
    tri_scr[...] = t_ref[...].astype(F32)
    for s in range(16):
        cells = _rows(p_ref, s).astype(F32)
        out = _finished(tri_scr, s, cells, _rows(g_ref, s), og_ref[...], ob_ref[...], ow_ref[...])
        _put_rows(out_ref, s, out)


def _pair_up(one, two):
    low = jnp.concatenate([one[..., :64], two[..., :64]], axis=-1)
    high = jnp.concatenate([one[..., 64:], two[..., 64:]], axis=-1)
    return low, high


def _outgoing_kernel(x_ref, in_ref, out_ref, l_scr, r_scr):
    for t, scr in ((0, l_scr), (1, r_scr)):
        for pair in range(2):
            low, high = _pair_up(in_ref[:, 2 * pair, t], in_ref[:, 2 * pair + 1, t])
            scr[:, 0, :, pair * 128 : pair * 128 + 128] = low
            scr[:, 1, :, pair * 128 : pair * 128 + 128] = high
    right = r_scr[...].reshape(1024, 256)
    here = x_ref[0]
    for part in range(4):
        left = l_scr[part * 8 : part * 8 + 8].reshape(256, 256)
        tri = lax.dot_general(left, right, (((1,), (1,)), ((), ())), preferred_element_type=F32)
        tri = tri.astype(BF16).reshape(8, 2, 16, 1024)
        for zlo in range(4):
            for pair in range(2):
                lanes = tri[..., zlo * 256 + pair * 128 : zlo * 256 + pair * 128 + 128]
                low, high = _pair_up(lanes[:, 0], lanes[:, 1])
                rows = slice(part * 8, part * 8 + 8)
                out_ref[(2 * pair - here) & 3, rows, zlo] = low
                out_ref[(2 * pair + 1 - here) & 3, rows, zlo] = high


def _incoming_kernel(
    x_ref, own_ref, before_ref, after_ref, far_a_ref, far_b_ref, r_ref, out_ref, l_scr, r_scr
):
    def load(scr, parts):
        base = 0
        for ref in parts:
            n = ref.shape[0]
            for pair in range(2):
                low, high = _pair_up(ref[:, 2 * pair], ref[:, 2 * pair + 1])
                lanes = slice(pair * 128, pair * 128 + 128)
                scr[0, base : base + n, :, lanes] = low
                scr[1, base : base + n, :, lanes] = high
            base += n

    load(r_scr, (r_ref,))
    right = r_scr[...].reshape(1024, 256)
    here = x_ref[0]
    for step, parts in ((0, (own_ref,)), (3, (before_ref,)), (1, (after_ref,)), (2, (far_a_ref, far_b_ref))):
        load(l_scr, parts)
        left = l_scr[...].reshape(1024, 256)
        tri = lax.dot_general(left, right, (((0,), (0,)), ((), ())), preferred_element_type=F32)
        tri = tri.astype(BF16).reshape(4, 2, 2, 16, 256)
        for pair in range(2):
            lanes = tri[..., pair * 128 : pair * 128 + 128]
            low, high = _pair_up(lanes[:, :, 0], lanes[:, :, 1])
            out_ref[:, (here + step) & 3, :, 2 * pair] = low
            out_ref[:, (here + step) & 3, :, 2 * pair + 1] = high


def _call(kernel, outs, scratch, args, mib=48, scalar=False):
    specs = [pl.BlockSpec(memory_space=pltpu.VMEM) for _ in args]
    if scalar:
        specs[0] = pl.BlockSpec(memory_space=pltpu.SMEM)
    return pl.pallas_call(
        kernel,
        out_shape=[jax.ShapeDtypeStruct(shape, dtype) for shape, dtype in outs],
        in_specs=specs,
        out_specs=[pl.BlockSpec(memory_space=pltpu.VMEM) for _ in outs],
        scratch_shapes=[pltpu.VMEM(shape, dtype) for shape, dtype in scratch],
        compiler_params=_params(mib),
    )(*args)


def _exchange(tiles):
    return lax.all_to_all(tiles, GROUP, split_axis=0, concat_axis=0, tiled=True)


def _shift(value, step):
    return lax.ppermute(value, "x", [(i, (i + step) % 4) for i in range(4)])


def _sum(*parts):
    total = parts[0].astype(F32)
    for part in parts[1:]:
        total = total + part.astype(F32)
    return total.astype(BF16)


def body(pair_rep, in_gain, in_bias, proj_w, gate_w, out_gain, out_bias, out_w):
    block = pair_rep.shape
    here = lax.axis_index("x").astype(jnp.int32).reshape(1)

    def row_of(value, u):
        return value[u].reshape(1, 128)

    def column_of(value, u):
        return value[u].reshape(128, 1)

    tiles, gate = _call(
        _first_kernel,
        [((4096, 128), BF16), (block, F32)],
        [((4096, 128), F32)],
        (pair_rep, row_of(in_gain, 0), row_of(in_bias, 0), proj_w[0], gate_w[0]),
    )
    both = _exchange(tiles.reshape(128, 32, 128)).reshape(32, 4, 2, 16, 128)
    (partial,) = _call(
        _outgoing_kernel,
        [((4, 32, 4, 16, 128), BF16)],
        [((32, 2, 16, 256), BF16), ((32, 2, 16, 256), BF16)],
        (here, both),
        scalar=True,
    )
    far_up = _shift(partial[2, :16], 1)
    far_down = _shift(partial[2, 16:], -1)
    up = jnp.concatenate([_sum(partial[1, :16], far_up), partial[1, 16:]], axis=0)
    down = jnp.concatenate([partial[3, :16], _sum(partial[3, 16:], far_down)], axis=0)
    tri = _sum(partial[0], _shift(up, 1), _shift(down, -1))
    tri = _exchange(tri.reshape(128, 16, 128))

    middle, left, right, gate = _call(
        _middle_kernel,
        [(block, BF16), ((2048, 128), BF16), ((2048, 128), BF16), (block, F32)],
        [((2048, 128), F32), ((2048, 128), F32), ((2048, 128), F32)],
        (
            tri.reshape(2048, 128), pair_rep, gate,
            column_of(out_gain, 0), column_of(out_bias, 0), out_w[0],
            row_of(in_gain, 1), row_of(in_bias, 1), proj_w[1], gate_w[1],
        ),
    )
    left = _exchange(left.reshape(128, 16, 128))
    left, right = lax.optimization_barrier((left, right))
    right = _exchange(right.reshape(128, 16, 128)).reshape(32, 4, 16, 128)
    left = left.reshape(32, 4, 16, 128)
    before = _shift(left, 1)
    after = _shift(left, -1)
    far_a = _shift(before[:16], 1)
    far_b = _shift(after[16:], -1)
    (tri,) = _call(
        _incoming_kernel,
        [((4, 4, 2, 4, 16, 128), BF16)],
        [((2, 32, 16, 256), BF16), ((2, 32, 16, 256), BF16)],
        (here, left, before, after, far_a, far_b, right),
        scalar=True,
    )
    tri = _exchange(tri.reshape(128, 16, 128))
    (out,) = _call(
        _last_kernel,
        [(block, BF16)],
        [((2048, 128), F32)],
        (
            tri.reshape(2048, 128), middle, gate,
            column_of(out_gain, 1), column_of(out_bias, 1), out_w[1],
        ),
    )
    return out


def solution(mesh):
    fine = Mesh(mesh.devices.reshape(2, 8, 2, 4, 4), ("zhi", "y", "core", "zlo", "x"))
    cells = P(("zhi", "y", "core"), ("zlo", "x"), None)
    placed = (cells, P(), P(), P(), P(), P(), P(), P())
    return jax.shard_map(body, mesh=fine, in_specs=placed, out_specs=cells, check_vma=False)
```

profile of v0, /device:TPU:6, one launch (start us, length us, event | category | flops | bytes accessed | tf_op | source)
XLA Modules:
  0.0 227.5 jit_solution(4673924127432648416)
XLA Ops:
  0.0 1.0 slice_bitcast_fusion.7
  2.5 1.0 copy-done
  3.6 4.2 %shard_map.82 = (bf16[4096,128]{1,0:T(8,128)(2,1)}, f32[32,64,128]{2,1,0:T(8,128)S(1)}) custom-call(bf16[32,64,128]{2,1,0:T(8,128)(2,1)S(1)} %copy-done, f32[1,128]{1,0:T(1,128)S(1)} %get-tuple-element.41.gain_ref, f32[1,128]{1,0:T(1,128)S(1)} %get-tuple-element.38.bias_ref, bf16[128,512]{1,0:T(8,128)(2,1)S(1)} %get-tuple-element.28.w_ref, ...), custom_call_target="tpu_custom_call" | custom-call | tf_op jit(solution)/shard_map/pallas_call | solution.py:155
  7.8 17.8 %all-to-all-start = ((bf16[128,32,128]{2,1,0:T(8,128)(2,1)}), bf16[128,32,128]{2,1,0:T(8,128)(2,1)S(1)}, u32[]{:S(2)}, u32[]{:S(2)}) async-start(bf16[128,32,128]{2,1,0:T(8,128)(2,1)} %bitcast.3), calls=%async_computation | async-start | bytes 2097152 | tf_op jit(solution)/shard_map/all_to_all | solution.py:166
  25.6 30.4 %all-to-all-done = bf16[128,32,128]{2,1,0:T(8,128)(2,1)S(1)} async-done(((bf16[128,32,128]{2,1,0:T(8,128)(2,1)}), bf16[128,32,128]{2,1,0:T(8,128)(2,1)S(1)}, u32[]{:S(2)}, u32[]{:S(2)}) %all-to-all-start) | async-done | bytes 1048608 | tf_op jit(solution)/shard_map/all_to_all | solution.py:166
  56.0 1.0 shard_map.83
  57.3 2.4 %collective-permute-start = (bf16[16,4,16,128]{3,2,1,0:T(8,128)(2,1)S(1)}, bf16[16,4,16,128]{3,2,1,0:T(8,128)(2,1)S(1)}, u32[]{:S(2)}, u32[]{:S(2)}) collective-permute-start(bf16[16,4,16,128]{3,2,1,0:T(8,128)(2,1)S(1)} %get-tuple-element.23), channel_id=1, source_target_pairs={{0,1},{1,2},{2,3},{3,0},{4,5},{5,6},{6,7},{7,4},{8,9},{9,10},{10,1... | collective-permute-start | bytes 786440 | tf_op jit(solution)/shard_map/ppermute | solution.py:170
  59.7 3.4 %collective-permute-start.2 = (bf16[16,4,16,128]{3,2,1,0:T(8,128)(2,1)S(1)}, bf16[16,4,16,128]{3,2,1,0:T(8,128)(2,1)S(1)}, u32[]{:S(2)}, u32[]{:S(2)}) collective-permute-start(bf16[16,4,16,128]{3,2,1,0:T(8,128)(2,1)S(1)} %get-tuple-element.24), channel_id=1, source_target_pairs={{0,3},{1,0},{2,1},{3,2},{4,7},{5,4},{6,5},{7,6},{8,11},{9,8},{10,9... | collective-permute-start | bytes 786440 | tf_op jit(solution)/shard_map/ppermute | solution.py:170
  63.1 4.2 %collective-permute-done = bf16[16,4,16,128]{3,2,1,0:T(8,128)(2,1)S(1)} collective-permute-done((bf16[16,4,16,128]{3,2,1,0:T(8,128)(2,1)S(1)}, bf16[16,4,16,128]{3,2,1,0:T(8,128)(2,1)S(1)}, u32[]{:S(2)}, u32[]{:S(2)}) %collective-permute-start) | collective-permute-done | bytes 262176 | tf_op jit(solution)/shard_map/ppermute | solution.py:170
  67.3 3.3 %collective-permute-done.2 = bf16[16,4,16,128]{3,2,1,0:T(8,128)(2,1)S(1)} collective-permute-done((bf16[16,4,16,128]{3,2,1,0:T(8,128)(2,1)S(1)}, bf16[16,4,16,128]{3,2,1,0:T(8,128)(2,1)S(1)}, u32[]{:S(2)}, u32[]{:S(2)}) %collective-permute-start.2) | collective-permute-done | bytes 262176 | tf_op jit(solution)/shard_map/ppermute | solution.py:170
  70.9 2.2 collective-permute-start.1
  73.2 3.8 %collective-permute-start.3 = (bf16[32,4,16,128]{3,2,1,0:T(8,128)(2,1)S(1)}, bf16[32,4,16,128]{3,2,1,0:T(8,128)(2,1)S(1)}, u32[]{:S(2)}, u32[]{:S(2)}) collective-permute-start(bf16[32,4,16,128]{3,2,1,0:T(8,128)(2,1)S(1)} %pad_maximum_fusion.1), channel_id=1, source_target_pairs={{0,3},{1,0},{2,1},{3,2},{4,7},{5,4},{6,5},{7,6},{8,11},{9,8},{10,9... | collective-permute-start | bytes 1572872 | tf_op jit(solution)/shard_map/ppermute | solution.py:170
  77.0 8.4 %collective-permute-done.1 = bf16[32,4,16,128]{3,2,1,0:T(8,128)(2,1)S(1)} collective-permute-done((bf16[32,4,16,128]{3,2,1,0:T(8,128)(2,1)S(1)}, bf16[32,4,16,128]{3,2,1,0:T(8,128)(2,1)S(1)}, u32[]{:S(2)}, u32[]{:S(2)}) %collective-permute-start.1) | collective-permute-done | bytes 524320 | tf_op jit(solution)/shard_map/ppermute | solution.py:170
  85.3 3.4 %collective-permute-done.3 = bf16[32,4,16,128]{3,2,1,0:T(8,128)(2,1)S(1)} collective-permute-done((bf16[32,4,16,128]{3,2,1,0:T(8,128)(2,1)S(1)}, bf16[32,4,16,128]{3,2,1,0:T(8,128)(2,1)S(1)}, u32[]{:S(2)}, u32[]{:S(2)}) %collective-permute-start.3) | collective-permute-done | bytes 524320 | tf_op jit(solution)/shard_map/ppermute | solution.py:170
  88.7 1.1 fusion.1
  89.8 7.8 %all-to-all-start.1 = ((bf16[128,16,128]{2,1,0:T(8,128)(2,1)}), bf16[128,16,128]{2,1,0:T(8,128)(2,1)S(1)}, u32[]{:S(2)}, u32[]{:S(2)}) async-start(bf16[128,16,128]{2,1,0:T(8,128)(2,1)} %bitcast.12), calls=%async_computation.1 | async-start | bytes 1048576 | tf_op jit(solution)/shard_map/all_to_all | solution.py:166
  98.7 18.8 %all-to-all-done.1 = bf16[128,16,128]{2,1,0:T(8,128)(2,1)S(1)} async-done(((bf16[128,16,128]{2,1,0:T(8,128)(2,1)}), bf16[128,16,128]{2,1,0:T(8,128)(2,1)S(1)}, u32[]{:S(2)}, u32[]{:S(2)}) %all-to-all-start.1) | async-done | bytes 524320 | tf_op jit(solution)/shard_map/all_to_all | solution.py:166
  117.5 6.3 %shard_map.84 = (bf16[32,64,128]{2,1,0:T(8,128)(2,1)S(1)}, bf16[2048,128]{1,0:T(8,128)(2,1)S(1)}, bf16[2048,128]{1,0:T(8,128)(2,1)S(1)}, f32[32,64,128]{2,1,0:T(8,128)S(1)}) custom-call(bf16[2048,128]{1,0:T(8,128)(2,1)S(1)} %bitcast.59, bf16[32,64,128]{2,1,0:T(8,128)(2,1)S(1)} %copy-done.1, f32[32,64,128]{2,1,0:T(8,128)S(1)} %get-tuple-element.14.g_ref, ...), custom_call_target="tpu_custom_call" | custom-call | tf_op jit(solution)/shard_map/pallas_call | solution.py:155
  123.8 25.9 %all_to_all.25 = bf16[128,16,128]{2,1,0:T(8,128)(2,1)S(1)} all-to-all(bf16[128,16,128]{2,1,0:T(8,128)(2,1)S(1)} %bitcast.62), channel_id=1, replica_groups=mesh['zhi'=2,'y'=8,'core'=2,'zlo'=4,'x'=4] {'zhi','y','core','zlo'}, dimensions={0} | all-to-all | bytes 1048576 | tf_op jit(solution)/shard_map/all_to_all | solution.py:166
  149.7 6.2 %all-to-all-start.3 = ((bf16[128,16,128]{2,1,0:T(8,128)(2,1)}), bf16[128,16,128]{2,1,0:T(8,128)(2,1)S(1)}, u32[]{:S(2)}, u32[]{:S(2)}) async-start(bf16[128,16,128]{2,1,0:T(8,128)(2,1)} %bitcast.61), calls=%async_computation.3 | async-start | bytes 1048576 | tf_op jit(solution)/shard_map/all_to_all | solution.py:166
  155.9 2.2 collective-permute-start.4
  158.1 3.6 %collective-permute-start.5 = (bf16[32,4,16,128]{3,2,1,0:T(8,128)(2,1)S(1)}, bf16[32,4,16,128]{3,2,1,0:T(8,128)(2,1)S(1)}, u32[]{:S(2)}, u32[]{:S(2)}) collective-permute-start(bf16[32,4,16,128]{3,2,1,0:T(8,128)(2,1)S(1)} %bitcast.56), channel_id=1, source_target_pairs={{0,3},{1,0},{2,1},{3,2},{4,7},{5,4},{6,5},{7,6},{8,11},{9,8},{10,9... | collective-permute-start | bytes 1572872 | tf_op jit(solution)/shard_map/ppermute | solution.py:170
  161.8 9.4 %collective-permute-done.4.before_ref = bf16[32,4,16,128]{3,2,1,0:T(8,128)(2,1)S(1)} collective-permute-done((bf16[32,4,16,128]{3,2,1,0:T(8,128)(2,1)S(1)}, bf16[32,4,16,128]{3,2,1,0:T(8,128)(2,1)S(1)}, u32[]{:S(2)}, u32[]{:S(2)}) %collective-permute-start.4) | collective-permute-done | bytes 524320 | tf_op jit(solution)/shard_map/ppermute | solution.py:170
  171.2 3.4 %collective-permute-start.6 = (bf16[16,4,16,128]{3,2,1,0:T(8,128)(2,1)S(1)}, bf16[16,4,16,128]{3,2,1,0:T(8,128)(2,1)S(1)}, u32[]{:S(2)}, u32[]{:S(2)}) collective-permute-start(bf16[16,4,16,128]{3,2,1,0:T(8,128)(2,1)S(1)} %slice.99), channel_id=1, source_target_pairs={{0,1},{1,2},{2,3},{3,0},{4,5},{5,6},{6,7},{7,4},{8,9},{9,10},{10,1... | collective-permute-start | bytes 786440 | tf_op jit(solution)/shard_map/ppermute | solution.py:170
  174.7 2.4 %collective-permute-start.7 = (bf16[16,4,16,128]{3,2,1,0:T(8,128)(2,1)S(1)}, bf16[16,4,16,128]{3,2,1,0:T(8,128)(2,1)S(1)}, u32[]{:S(2)}, u32[]{:S(2)}) collective-permute-start(bf16[16,4,16,128]{3,2,1,0:T(8,128)(2,1)S(1)} %slice.100), channel_id=1, source_target_pairs={{0,3},{1,0},{2,1},{3,2},{4,7},{5,4},{6,5},{7,6},{8,11},{9,8},{10,9... | collective-permute-start | bytes 786440 | tf_op jit(solution)/shard_map/ppermute | solution.py:170
  177.1 2.8 %collective-permute-done.6.far_a_ref = bf16[16,4,16,128]{3,2,1,0:T(8,128)(2,1)S(1)} collective-permute-done((bf16[16,4,16,128]{3,2,1,0:T(8,128)(2,1)S(1)}, bf16[16,4,16,128]{3,2,1,0:T(8,128)(2,1)S(1)}, u32[]{:S(2)}, u32[]{:S(2)}) %collective-permute-start.6) | collective-permute-done | bytes 262176 | tf_op jit(solution)/shard_map/ppermute | solution.py:170
  179.9 4.4 %collective-permute-done.7.far_b_ref = bf16[16,4,16,128]{3,2,1,0:T(8,128)(2,1)S(1)} collective-permute-done((bf16[16,4,16,128]{3,2,1,0:T(8,128)(2,1)S(1)}, bf16[16,4,16,128]{3,2,1,0:T(8,128)(2,1)S(1)}, u32[]{:S(2)}, u32[]{:S(2)}) %collective-permute-start.7) | collective-permute-done | bytes 262176 | tf_op jit(solution)/shard_map/ppermute | solution.py:170
  186.0 3.1 %shard_map.85 = bf16[4,4,2,4,16,128]{5,4,3,2,1,0:T(8,128)(2,1)} custom-call(s32[1]{0:T(128)} %bitcast.x_ref, bf16[32,4,16,128]{3,2,1,0:T(8,128)(2,1)S(1)} %bitcast.57, bf16[32,4,16,128]{3,2,1,0:T(8,128)(2,1)S(1)} %collective-permute-done.4.before_ref, bf16[32,4,16,128]{3,2,1,0:T(8,128)(2,1)S(1)} %collective-permute-done.5.after_ref, ...), custom_call_target="tpu_custom_call" | custom-call | tf_op jit(solution)/shard_map/pallas_call | solution.py:155
  189.1 15.2 %all-to-all-start.4 = ((bf16[128,16,128]{2,1,0:T(8,128)(2,1)}), bf16[128,16,128]{2,1,0:T(8,128)(2,1)S(1)}, u32[]{:S(2)}, u32[]{:S(2)}) async-start(bf16[128,16,128]{2,1,0:T(8,128)(2,1)} %bitcast.23), calls=%async_computation.4 | async-start | bytes 1048576 | tf_op jit(solution)/shard_map/all_to_all | solution.py:166
  204.5 19.8 %all-to-all-done.4 = bf16[128,16,128]{2,1,0:T(8,128)(2,1)S(1)} async-done(((bf16[128,16,128]{2,1,0:T(8,128)(2,1)}), bf16[128,16,128]{2,1,0:T(8,128)(2,1)S(1)}, u32[]{:S(2)}, u32[]{:S(2)}) %all-to-all-start.4) | async-done | bytes 524320 | tf_op jit(solution)/shard_map/all_to_all | solution.py:166
  224.3 1.0 copy-done.4
  225.4 2.1 shard_map.86
  (33 shorter events, 5.0 us)
Async XLA Ops:
  2.5 1.0 copy-start
  7.8 48.2 %all-to-all-start = ((bf16[128,32,128]{2,1,0:T(8,128)(2,1)}), bf16[128,32,128]{2,1,0:T(8,128)(2,1)S(1)}, u32[]{:S(2)}, u32[]{:S(2)}) async-start(bf16[128,32,128]{2,1,0:T(8,128)(2,1)} %bitcast.3), calls=%async_computation | async-start | bytes 2097152 | tf_op jit(solution)/shard_map/all_to_all | solution.py:166
  57.3 10.0 %collective-permute-start = (bf16[16,4,16,128]{3,2,1,0:T(8,128)(2,1)S(1)}, bf16[16,4,16,128]{3,2,1,0:T(8,128)(2,1)S(1)}, u32[]{:S(2)}, u32[]{:S(2)}) collective-permute-start(bf16[16,4,16,128]{3,2,1,0:T(8,128)(2,1)S(1)} %get-tuple-element.23), channel_id=1, source_target_pairs={{0,1},{1,2},{2,3},{3,0},{4,5},{5,6},{6,7},{7,4},{8,9},{9,10},{10,1... | collective-permute-start | bytes 786440 | tf_op jit(solution)/shard_map/ppermute | solution.py:170
  59.7 11.0 %collective-permute-start.2 = (bf16[16,4,16,128]{3,2,1,0:T(8,128)(2,1)S(1)}, bf16[16,4,16,128]{3,2,1,0:T(8,128)(2,1)S(1)}, u32[]{:S(2)}, u32[]{:S(2)}) collective-permute-start(bf16[16,4,16,128]{3,2,1,0:T(8,128)(2,1)S(1)} %get-tuple-element.24), channel_id=1, source_target_pairs={{0,3},{1,0},{2,1},{3,2},{4,7},{5,4},{6,5},{7,6},{8,11},{9,8},{10,9... | collective-permute-start | bytes 786440 | tf_op jit(solution)/shard_map/ppermute | solution.py:170
  70.9 14.5 %collective-permute-start.1 = (bf16[32,4,16,128]{3,2,1,0:T(8,128)(2,1)S(1)}, bf16[32,4,16,128]{3,2,1,0:T(8,128)(2,1)S(1)}, u32[]{:S(2)}, u32[]{:S(2)}) collective-permute-start(bf16[32,4,16,128]{3,2,1,0:T(8,128)(2,1)S(1)} %pad_maximum_fusion), channel_id=1, source_target_pairs={{0,1},{1,2},{2,3},{3,0},{4,5},{5,6},{6,7},{7,4},{8,9},{9,10},{10,1... | collective-permute-start | bytes 1572872 | tf_op jit(solution)/shard_map/ppermute | solution.py:170
  73.1 24.5 %copy-start.7 = (f32[2,128]{1,0:T(2,128)S(1)}, f32[2,128]{1,0:T(2,128)}, u32[]{:S(2)}) copy-start(f32[2,128]{1,0:T(2,128)} %param.14) | copy-start | bytes 3076
  73.1 24.7 %copy-start.8 = (f32[2,128]{1,0:T(2,128)S(1)}, f32[2,128]{1,0:T(2,128)}, u32[]{:S(2)}) copy-start(f32[2,128]{1,0:T(2,128)} %param.13) | copy-start | bytes 3076
  73.1 44.4 %copy-start.1 = (bf16[32,64,128]{2,1,0:T(8,128)(2,1)S(1)}, bf16[32,64,128]{2,1,0:T(8,128)(2,1)}, u32[]{:S(2)}) copy-start(bf16[32,64,128]{2,1,0:T(8,128)(2,1)} %p_ref.3) | copy-start | bytes 1572868
  73.2 15.5 %collective-permute-start.3 = (bf16[32,4,16,128]{3,2,1,0:T(8,128)(2,1)S(1)}, bf16[32,4,16,128]{3,2,1,0:T(8,128)(2,1)S(1)}, u32[]{:S(2)}, u32[]{:S(2)}) collective-permute-start(bf16[32,4,16,128]{3,2,1,0:T(8,128)(2,1)S(1)} %pad_maximum_fusion.1), channel_id=1, source_target_pairs={{0,3},{1,0},{2,1},{3,2},{4,7},{5,4},{6,5},{7,6},{8,11},{9,8},{10,9... | collective-permute-start | bytes 1572872 | tf_op jit(solution)/shard_map/ppermute | solution.py:170
  89.8 27.7 %all-to-all-start.1 = ((bf16[128,16,128]{2,1,0:T(8,128)(2,1)}), bf16[128,16,128]{2,1,0:T(8,128)(2,1)S(1)}, u32[]{:S(2)}, u32[]{:S(2)}) async-start(bf16[128,16,128]{2,1,0:T(8,128)(2,1)} %bitcast.12), calls=%async_computation.1 | async-start | bytes 1048576 | tf_op jit(solution)/shard_map/all_to_all | solution.py:166
  123.8 25.9 %copy-start.3 = (bf16[32,64,128]{2,1,0:T(8,128)(2,1)}, bf16[32,64,128]{2,1,0:T(8,128)(2,1)S(1)}, u32[]{:S(2)}) copy-start(bf16[32,64,128]{2,1,0:T(8,128)(2,1)S(1)} %get-tuple-element.19.p_ref) | copy-start | bytes 1572868
  123.8 25.9 %copy-start.2 = (bf16[2048,128]{1,0:T(8,128)(2,1)}, bf16[2048,128]{1,0:T(8,128)(2,1)S(1)}, u32[]{:S(2)}) copy-start(bf16[2048,128]{1,0:T(8,128)(2,1)S(1)} %get-tuple-element.18) | copy-start | bytes 1572868
  149.7 35.3 %all-to-all-start.3 = ((bf16[128,16,128]{2,1,0:T(8,128)(2,1)}), bf16[128,16,128]{2,1,0:T(8,128)(2,1)S(1)}, u32[]{:S(2)}, u32[]{:S(2)}) async-start(bf16[128,16,128]{2,1,0:T(8,128)(2,1)} %bitcast.61), calls=%async_computation.3 | async-start | bytes 1048576 | tf_op jit(solution)/shard_map/all_to_all | solution.py:166
  155.9 15.2 %collective-permute-start.4 = (bf16[32,4,16,128]{3,2,1,0:T(8,128)(2,1)S(1)}, bf16[32,4,16,128]{3,2,1,0:T(8,128)(2,1)S(1)}, u32[]{:S(2)}, u32[]{:S(2)}) collective-permute-start(bf16[32,4,16,128]{3,2,1,0:T(8,128)(2,1)S(1)} %bitcast.55), channel_id=1, source_target_pairs={{0,1},{1,2},{2,3},{3,0},{4,5},{5,6},{6,7},{7,4},{8,9},{9,10},{10,1... | collective-permute-start | bytes 1572872 | tf_op jit(solution)/shard_map/ppermute | solution.py:170
  158.1 16.5 %collective-permute-start.5 = (bf16[32,4,16,128]{3,2,1,0:T(8,128)(2,1)S(1)}, bf16[32,4,16,128]{3,2,1,0:T(8,128)(2,1)S(1)}, u32[]{:S(2)}, u32[]{:S(2)}) collective-permute-start(bf16[32,4,16,128]{3,2,1,0:T(8,128)(2,1)S(1)} %bitcast.56), channel_id=1, source_target_pairs={{0,3},{1,0},{2,1},{3,2},{4,7},{5,4},{6,5},{7,6},{8,11},{9,8},{10,9... | collective-permute-start | bytes 1572872 | tf_op jit(solution)/shard_map/ppermute | solution.py:170
  171.2 8.7 %collective-permute-start.6 = (bf16[16,4,16,128]{3,2,1,0:T(8,128)(2,1)S(1)}, bf16[16,4,16,128]{3,2,1,0:T(8,128)(2,1)S(1)}, u32[]{:S(2)}, u32[]{:S(2)}) collective-permute-start(bf16[16,4,16,128]{3,2,1,0:T(8,128)(2,1)S(1)} %slice.99), channel_id=1, source_target_pairs={{0,1},{1,2},{2,3},{3,0},{4,5},{5,6},{6,7},{7,4},{8,9},{9,10},{10,1... | collective-permute-start | bytes 786440 | tf_op jit(solution)/shard_map/ppermute | solution.py:170
  174.7 9.6 %collective-permute-start.7 = (bf16[16,4,16,128]{3,2,1,0:T(8,128)(2,1)S(1)}, bf16[16,4,16,128]{3,2,1,0:T(8,128)(2,1)S(1)}, u32[]{:S(2)}, u32[]{:S(2)}) collective-permute-start(bf16[16,4,16,128]{3,2,1,0:T(8,128)(2,1)S(1)} %slice.100), channel_id=1, source_target_pairs={{0,3},{1,0},{2,1},{3,2},{4,7},{5,4},{6,5},{7,6},{8,11},{9,8},{10,9... | collective-permute-start | bytes 786440 | tf_op jit(solution)/shard_map/ppermute | solution.py:170
  184.3 0.7 copy-start.5
  185.0 1.0 copy-start.6
  189.1 35.3 %all-to-all-start.4 = ((bf16[128,16,128]{2,1,0:T(8,128)(2,1)}), bf16[128,16,128]{2,1,0:T(8,128)(2,1)S(1)}, u32[]{:S(2)}, u32[]{:S(2)}) async-start(bf16[128,16,128]{2,1,0:T(8,128)(2,1)} %bitcast.23), calls=%async_computation.4 | async-start | bytes 1048576 | tf_op jit(solution)/shard_map/all_to_all | solution.py:166
  224.3 1.0 copy-start.4
where the time goes:
time: 228 us; the launch traced here: 227 us
  waiting for transfers between devices  105 us (46%)
  starting transfers between devices  70.6 us (31%)
  blocking collectives  25.9 us (11%)
  Pallas kernels  16.8 us (7%)
  local copies, waits for them, and re-layouts  7.77 us (3%)
    all_to_all x4, waiting for transfers between devices, _exchange(): return lax.all_to_all(tiles, GROUP, split_axis=0, concat_axis=0, tiled=True)  69 us
    all_to_all x4, starting transfers between devices, _exchange(): return lax.all_to_all(tiles, GROUP, split_axis=0, concat_axis=0, tiled=True)  47.1 us
    ppermute x8, waiting for transfers between devices, _shift(): return lax.ppermute(value, 'x', [(i, (i + step) % 4) for i in range(4)])  35.8 us
    all_to_all x1, blocking collectives, _exchange(): return lax.all_to_all(tiles, GROUP, split_axis=0, concat_axis=0, tiled=True)  25.9 us
    ppermute x8, starting transfers between devices, _shift(): return lax.ppermute(value, 'x', [(i, (i + step) % 4) for i in range(4)])  23.5 us
    pallas_call x5, Pallas kernels, _call(): pl.pallas_call(kernel, out_shape=[jax.ShapeDtypeStruct(shape, dtype) for...  16.8 us
  transfers between devices with their start and end apart: 12, of which 10 were waited for; matrix products, arithmetic and copies ran while one was open for 1% of the time, Pallas kernels for 0%

commit v1 on v0

v1 whole, which is shorter than its diff:
```python
import jax
import jax.numpy as jnp
from jax import lax
from jax.experimental import pallas as pl
from jax.experimental.pallas import tpu as pltpu
from jax.sharding import Mesh
from jax.sharding import PartitionSpec as P

GROUP = ("zhi", "y", "zlo", "x")
EPS = 1e-05
F32 = jnp.float32
BF16 = jnp.bfloat16


def _norm(values, axis, gain, bias):
    center = values - jnp.mean(values, axis=axis, keepdims=True)
    spread = jnp.mean(center * center, axis=axis, keepdims=True)
    return center * lax.rsqrt(spread + EPS) * gain + bias


def _project(cells, gain, bias, turned_w, gate_w):
    normed = _norm(cells, 1, gain, bias).astype(BF16)
    halves = lax.dot_general(
        turned_w, normed, (((1,), (1,)), ((), ())), preferred_element_type=F32
    )
    left = jax.nn.sigmoid(halves[128:256]) * halves[:128]
    right = jax.nn.sigmoid(halves[384:]) * halves[256:384]
    gate = jax.nn.sigmoid(jnp.dot(normed, gate_w, preferred_element_type=F32))
    return left, right, gate


def _pair_up(one, two):
    low = jnp.concatenate([one[..., :64], two[..., :64]], axis=-1)
    high = jnp.concatenate([one[..., 64:], two[..., 64:]], axis=-1)
    return low, high


def _quarter(parts, q):
    return jnp.concatenate([part[..., 32 * q : 32 * q + 32] for part in parts], axis=-1)


def _rows(ref, s):
    return jnp.concatenate([ref[s], ref[16 + s]], axis=0)


def _put_rows(ref, s, value):
    ref[s] = value[:64]
    ref[16 + s] = value[64:]


def _put_operands(scr, s, left, right):
    low, high = _pair_up(left, right)
    scr[pl.ds(s, 128, stride=32), :] = low
    scr[pl.ds(16 + s, 128, stride=32), :] = high


def _column(ref, u):
    return jnp.broadcast_to(ref[u : u + 1, :], (128, 128)).T


def _first_kernel(p_ref, gain_ref, bias_ref, w_ref, gw_ref, out_ref, gate_ref, scr):
    turned_w = w_ref[0].T
    for s in range(16):
        cells = jnp.concatenate(
            [p_ref[s, :32], p_ref[16 + s, :32], p_ref[s, 32:], p_ref[16 + s, 32:]], axis=0
        ).astype(F32)
        left, right, gate = _project(cells, gain_ref[:1], bias_ref[:1], turned_w, gw_ref[0])
        _put_operands(scr, s, left, right)
        gate_ref[s, :32] = gate[:32]
        gate_ref[16 + s, :32] = gate[32:64]
        gate_ref[s, 32:] = gate[64:96]
        gate_ref[16 + s, 32:] = gate[96:]
    out_ref[...] = scr[...].astype(BF16)


def _load_products(t_ref, scr):
    total = t_ref[:, 0].astype(F32) + t_ref[:, 1].astype(F32)
    scr[...] = total.reshape(2048, 128)


def _finished(scr, s, cells, gate, gain, bias, out_w):
    tri = scr[pl.ds(s, 128, stride=16), :]
    mixed = _norm(tri, 0, gain, bias).astype(BF16)
    projected = lax.dot_general(
        mixed, out_w, (((0,), (0,)), ((), ())), preferred_element_type=F32
    )
    return (cells + gate * projected).astype(BF16)


def _middle_kernel(
    t_ref, p_ref, g_ref, og_ref, ob_ref, ow_ref, gain_ref, bias_ref, w_ref, gw_ref,
    mid_ref, out_ref, gate_ref, tri_scr, scr,
):
    _load_products(t_ref, tri_scr)
    turned_w = w_ref[1].T
    out_gain, out_bias = _column(og_ref, 0), _column(ob_ref, 0)
    for s in range(16):
        cells = _rows(p_ref, s).astype(F32)
        mid = _finished(tri_scr, s, cells, _rows(g_ref, s), out_gain, out_bias, ow_ref[0])
        _put_rows(mid_ref, s, mid)
        left, right, gate = _project(
            mid.astype(F32), gain_ref[1:], bias_ref[1:], turned_w, gw_ref[1]
        )
        _put_operands(scr, s, left, right)
        _put_rows(gate_ref, s, gate)
    out_ref[...] = scr[...].astype(BF16)


def _last_kernel(t_ref, p_ref, g_ref, og_ref, ob_ref, ow_ref, out_ref, tri_scr):
    _load_products(t_ref, tri_scr)
    out_gain, out_bias = _column(og_ref, 1), _column(ob_ref, 1)
    for s in range(16):
        cells = _rows(p_ref, s).astype(F32)
        out = _finished(tri_scr, s, cells, _rows(g_ref, s), out_gain, out_bias, ow_ref[1])
        _put_rows(out_ref, s, out)


def _put_products(out_ref, rows, tri):
    tri = tri.astype(BF16).reshape(-1, 2, 16, 1024)
    for pair in range(8):
        lanes = tri[..., pair * 128 : pair * 128 + 128]
        low, high = _pair_up(lanes[:, 0], lanes[:, 1])
        out_ref[rows, 2 * pair] = low
        out_ref[rows, 2 * pair + 1] = high


def _outgoing_kernel(core_ref, own_ref, other_ref, out_ref, l_scr, r_scr):
    core = core_ref[0]
    for zlo in range(4):
        lanes = slice(zlo * 128, zlo * 128 + 128)
        own = [own_ref[:, zlo * 4 + x] for x in range(4)]
        other = [other_ref[:, zlo * 4 + x] for x in range(4)]
        for b in range(2):
            l_scr[:, b, :, lanes] = _quarter(own, b)
            r_scr[:, pl.ds(core, 1), b, :, lanes] = _quarter(own, 2 + b)[:, None]
            r_scr[:, pl.ds(1 - core, 1), b, :, lanes] = _quarter(other, 2 + b)[:, None]
    right = r_scr[...].reshape(1024, 512)
    for part in range(2):
        rows = slice(part * 8, part * 8 + 8)
        left = l_scr[rows].reshape(256, 512)
        tri = lax.dot_general(left, right, (((1,), (1,)), ((), ())), preferred_element_type=F32)
        _put_products(out_ref, rows, tri)


def _incoming_kernel(core_ref, own_ref, other_ref, out_ref, l_scr, r_scr):
    first = core_ref[0] == 0
    for at, ref in ((0, own_ref), (1, other_ref)):
        for zlo in range(4):
            parts = [ref[:, zlo * 4 + x] for x in range(4)]
            lanes = slice(zlo * 128, zlo * 128 + 128)
            l_scr[at, :, :, lanes] = jnp.where(first, _quarter(parts, 0), _quarter(parts, 1))
            for pair in range(2):
                _, high = _pair_up(parts[2 * pair], parts[2 * pair + 1])
                start = zlo * 256 + pair * 128
                r_scr[at, :, :, start : start + 128] = high
    right = r_scr[...].reshape(512, 1024)
    for part in range(2):
        left = l_scr[:, :, :, part * 256 : part * 256 + 256].reshape(512, 256)
        tri = lax.dot_general(left, right, (((0,), (0,)), ((), ())), preferred_element_type=F32)
        _put_products(out_ref, slice(part * 8, part * 8 + 8), tri)


def _call(kernel, outs, scratch, args, scalar=False):
    specs = [pl.BlockSpec(memory_space=pltpu.VMEM) for _ in args]
    if scalar:
        specs[0] = pl.BlockSpec(memory_space=pltpu.SMEM)
    return pl.pallas_call(
        kernel,
        out_shape=[jax.ShapeDtypeStruct(shape, dtype) for shape, dtype in outs],
        in_specs=specs,
        out_specs=[pl.BlockSpec(memory_space=pltpu.VMEM) for _ in outs],
        scratch_shapes=[pltpu.VMEM(shape, dtype) for shape, dtype in scratch],
        compiler_params=pltpu.CompilerParams(vmem_limit_bytes=40 << 20),
    )(*args)


def _exchange(tiles):
    return lax.all_to_all(
        tiles.reshape(256, 16, 128), GROUP, split_axis=0, concat_axis=0, tiled=True
    )


def _products(kernel, scratch, tiles, core):
    own = _exchange(tiles).reshape(16, 16, 16, 128)
    other = lax.ppermute(own, "core", [(0, 1), (1, 0)])
    (out,) = _call(
        kernel, [((16, 16, 16, 128), BF16)], scratch, (core, own, other), scalar=True
    )
    return _exchange(out).reshape(128, 2, 16, 128)


def body(pair_rep, in_gain, in_bias, proj_w, gate_w, out_gain, out_bias, out_w):
    block = pair_rep.shape
    core = lax.axis_index("core").astype(jnp.int32).reshape(1)
    tiles, gate = _call(
        _first_kernel,
        [((4096, 128), BF16), (block, F32)],
        [((4096, 128), F32)],
        (pair_rep, in_gain, in_bias, proj_w, gate_w),
    )
    tri = _products(
        _outgoing_kernel,
        [((16, 2, 16, 512), BF16), ((16, 2, 2, 16, 512), BF16)],
        tiles,
        core,
    )
    middle, tiles, gate = _call(
        _middle_kernel,
        [(block, BF16), ((4096, 128), BF16), (block, F32)],
        [((2048, 128), F32), ((4096, 128), F32)],
        (tri, pair_rep, gate, out_gain, out_bias, out_w, in_gain, in_bias, proj_w, gate_w),
    )
    tri = _products(
        _incoming_kernel,
        [((2, 16, 16, 512), BF16), ((2, 16, 16, 1024), BF16)],
        tiles,
        core,
    )
    (out,) = _call(
        _last_kernel,
        [(block, BF16)],
        [((2048, 128), F32)],
        (tri, middle, gate, out_gain, out_bias, out_w),
    )
    return out


def solution(mesh):
    fine = Mesh(mesh.devices.reshape(2, 8, 2, 4, 4), ("zhi", "y", "core", "zlo", "x"))
    cells = P(("zhi", "y", "core"), ("zlo", "x"), None)
    placed = (cells, P(), P(), P(), P(), P(), P(), P())
    return jax.shard_map(body, mesh=fine, in_specs=placed, out_specs=cells, check_vma=False)
```

time: 228 us -> 207 us (0.908)
  blocking collectives: 25.9 us -> 174 us
  waiting for transfers between devices: 105 us -> 5.25 us
  starting transfers between devices: 70.6 us -> 3.82 us
  local copies, waits for them, and re-layouts: 7.77 us -> 4.86 us
    all_to_all x1 -> x4, blocking collectives: 25.9 us -> 174 us  [_exchange(): lax.all_to_all(tiles.reshape(256, 16, 128), GROUP, split_axis=0, concat_a...]
    all_to_all x4 -> x0, waiting for transfers between devices: 69 us -> none  [_exchange(): return lax.all_to_all(tiles, GROUP, split_axis=0, concat_axis=0, tiled=True)]
    all_to_all x4 -> x0, starting transfers between devices: 47.1 us -> none  [_exchange(): return lax.all_to_all(tiles, GROUP, split_axis=0, concat_axis=0, tiled=True)]
    ppermute x8 -> x2, waiting for transfers between devices: 35.8 us -> 5.25 us  [_products(): other = lax.ppermute(own, 'core', [(0, 1), (1, 0)])]
    ppermute x8 -> x2, starting transfers between devices: 23.5 us -> 3.82 us  [_products(): other = lax.ppermute(own, 'core', [(0, 1), (1, 0)])]
    squeeze x4 -> x0, local copies, waits for them, and re-layouts: 2.75 us -> none  [the longest x1 0.98 us: body(): proj_w[1]]
    unnamed x18 -> x26, local copies, waits for them, and re-layouts: 3.77 us -> 4.86 us
  transfers between devices with their start and end apart: 12 -> 2, of which waited for: 10 -> 2; matrix products, arithmetic and copies ran while one was open for 1% -> 0% of each run, Pallas kernels for 0% -> 0%
where the time goes in v1:
time: 207 us; the launch traced here: 205 us
  blocking collectives  174 us (84%)
  Pallas kernels  16.7 us (8%)
  waiting for transfers between devices  5.25 us (3%)
  local copies, waits for them, and re-layouts  4.86 us (2%)
  starting transfers between devices  3.82 us (2%)
    all_to_all x4, blocking collectives, _exchange(): lax.all_to_all(tiles.reshape(256, 16, 128), GROUP, split_axis=0, concat_a...  174 us
    pallas_call x5, Pallas kernels, _call(): pl.pallas_call(kernel, out_shape=[jax.ShapeDtypeStruct(shape, dtype) for...  16.7 us
    ppermute x2, waiting for transfers between devices, _products(): other = lax.ppermute(own, 'core', [(0, 1), (1, 0)])  5.25 us
    unnamed x26, local copies, waits for them, and re-layouts  4.86 us
  transfers between devices with their start and end apart: 2, of which 2 were waited for; matrix products, arithmetic and copies ran while one was open for 0% of the time, Pallas kernels for 0%

profile of v1, /device:TPU:6, one launch (start us, length us, event | category | flops | bytes accessed | tf_op | source)
XLA Modules:
  0.0 204.9 jit_solution(16067609392458557496)
XLA Ops:
  0.0 1.0 copy-done
  1.0 0.9 copy-done.2
  2.0 0.8 copy-done.5
  2.8 0.7 copy-done.7
  3.5 0.7 copy-done.9
  4.2 4.0 %shard_map.82 = (bf16[4096,128]{1,0:T(8,128)(2,1)S(1)}, f32[32,64,128]{2,1,0:T(8,128)S(1)}) custom-call(bf16[32,64,128]{2,1,0:T(8,128)(2,1)S(1)} %copy-done, f32[2,128]{1,0:T(2,128)S(1)} %copy-done.7, f32[2,128]{1,0:T(2,128)S(1)} %copy-done.9, bf16[2,128,512]{2,1,0:T(8,128)(2,1)S(1)} %copy-done.2, bf16[2,128,128]{2,1,0:T(8,128)(2,1)S(1)} %copy-done.5), custom_call_target="tpu_custom_call" | custom-call | tf_op jit(solution)/shard_map/pallas_call | solution.py:167
  8.2 51.6 %all_to_all.20 = bf16[256,16,128]{2,1,0:T(8,128)(2,1)S(1)} all-to-all(bf16[256,16,128]{2,1,0:T(8,128)(2,1)S(1)} %bitcast.18), channel_id=1, replica_groups=mesh['zhi'=2,'y'=8,'core'=2,'zlo'=4,'x'=4] {'zhi','y','zlo','x'}, dimensions={0} | all-to-all | bytes 2097152 | tf_op jit(solution)/shard_map/all_to_all | solution.py:178
  59.7 1.9 collective-permute-start
  61.7 2.6 %collective-permute-done.other_ref = bf16[16,16,16,128]{3,2,1,0:T(8,128)(2,1)S(1)} collective-permute-done((bf16[16,16,16,128]{3,2,1,0:T(8,128)(2,1)S(1)}, bf16[16,16,16,128]{3,2,1,0:T(8,128)(2,1)S(1)}, u32[]{:S(2)}, u32[]{:S(2)}) %collective-permute-start) | collective-permute-done | bytes 1048608 | tf_op jit(solution)/shard_map/ppermute | solution.py:185
  64.3 2.0 shard_map.83
  66.3 0.0 copy-start.1
  66.3 0.0 copy-start.3
  66.3 0.0 copy-start.4
  66.3 0.0 copy-start.6
  66.4 0.0 copy-start.10
  66.4 0.0 copy-start.11
  66.4 0.0 copy-start.12
  66.4 41.3 %all_to_all.21 = bf16[256,16,128]{2,1,0:T(8,128)(2,1)S(1)} all-to-all(bf16[256,16,128]{2,1,0:T(8,128)(2,1)S(1)} %bitcast.15), channel_id=1, replica_groups=mesh['zhi'=2,'y'=8,'core'=2,'zlo'=4,'x'=4] {'zhi','y','zlo','x'}, dimensions={0} | all-to-all | bytes 2097152 | tf_op jit(solution)/shard_map/all_to_all | solution.py:178
  107.7 0.0 copy-done.1
  107.7 0.0 copy-done.3
  107.7 0.0 copy-done.4
  107.7 0.0 copy-done.6
  107.7 0.0 copy-done.10
  107.7 0.0 copy-done.11
  107.7 0.6 copy-done.8
  108.4 7.0 %shard_map.84 = (bf16[32,64,128]{2,1,0:T(8,128)(2,1)S(1)}, bf16[4096,128]{1,0:T(8,128)(2,1)S(1)}, f32[32,64,128]{2,1,0:T(8,128)S(1)}) custom-call(bf16[128,2,16,128]{3,2,1,0:T(8,128)(2,1)S(1)} %bitcast.13, bf16[32,64,128]{2,1,0:T(8,128)(2,1)S(1)} %copy-done.1, f32[32,64,128]{2,1,0:T(8,128)S(1)} %get-tuple-element.11.g_ref, f32[2,128]{1,0:T(2,128)S(1)} %copy-done.11, ...), custom_call_target="tpu_custom_call" | custom-call | tf_op jit(solution)/shard_map/pallas_call | solution.py:167
  115.4 39.9 %all_to_all.22 = bf16[256,16,128]{2,1,0:T(8,128)(2,1)S(1)} all-to-all(bf16[256,16,128]{2,1,0:T(8,128)(2,1)S(1)} %bitcast.17), channel_id=1, replica_groups=mesh['zhi'=2,'y'=8,'core'=2,'zlo'=4,'x'=4] {'zhi','y','zlo','x'}, dimensions={0} | all-to-all | bytes 2097152 | tf_op jit(solution)/shard_map/all_to_all | solution.py:178
  155.4 1.9 collective-permute-start.1
  157.3 2.6 %collective-permute-done.1.other_ref = bf16[16,16,16,128]{3,2,1,0:T(8,128)(2,1)S(1)} collective-permute-done((bf16[16,16,16,128]{3,2,1,0:T(8,128)(2,1)S(1)}, bf16[16,16,16,128]{3,2,1,0:T(8,128)(2,1)S(1)}, u32[]{:S(2)}, u32[]{:S(2)}) %collective-permute-start.1) | collective-permute-done | bytes 1048608 | tf_op jit(solution)/shard_map/ppermute | solution.py:185
  159.9 1.8 shard_map.85
  161.8 41.3 %all_to_all.23 = bf16[256,16,128]{2,1,0:T(8,128)(2,1)S(1)} all-to-all(bf16[256,16,128]{2,1,0:T(8,128)(2,1)S(1)} %bitcast.14), channel_id=1, replica_groups=mesh['zhi'=2,'y'=8,'core'=2,'zlo'=4,'x'=4] {'zhi','y','zlo','x'}, dimensions={0} | all-to-all | bytes 2097152 | tf_op jit(solution)/shard_map/all_to_all | solution.py:178
  203.0 1.9 shard_map.86
  (7 shorter events, 0.0 us)
Async XLA Ops:
  0.0 1.0 copy-start
  1.0 0.9 copy-start.2
  2.0 0.8 copy-start.5
  2.8 0.7 copy-start.7
  3.5 0.7 copy-start.9
  59.7 4.5 %collective-permute-start = (bf16[16,16,16,128]{3,2,1,0:T(8,128)(2,1)S(1)}, bf16[16,16,16,128]{3,2,1,0:T(8,128)(2,1)S(1)}, u32[]{:S(2)}, u32[]{:S(2)}) collective-permute-start(bf16[16,16,16,128]{3,2,1,0:T(8,128)(2,1)S(1)} %bitcast.9), channel_id=1, source_target_pairs={{0,16},{16,0},{1,17},{17,1},{2,18},{18,2},{3,19},{19,3},{4,20},{20... | collective-permute-start | bytes 3145736 | tf_op jit(solution)/shard_map/ppermute | solution.py:185
  66.3 41.4 %copy-start.1 = (bf16[32,64,128]{2,1,0:T(8,128)(2,1)S(1)}, bf16[32,64,128]{2,1,0:T(8,128)(2,1)}, u32[]{:S(2)}) copy-start(bf16[32,64,128]{2,1,0:T(8,128)(2,1)} %p_ref.3) | copy-start | bytes 1572868
  66.3 41.4 %copy-start.3 = (bf16[2,128,512]{2,1,0:T(8,128)(2,1)S(1)}, bf16[2,128,512]{2,1,0:T(8,128)(2,1)}, u32[]{:S(2)}) copy-start(bf16[2,128,512]{2,1,0:T(8,128)(2,1)} %w_ref.3) | copy-start | bytes 786436
  66.3 41.4 %copy-start.4 = (bf16[2,128,128]{2,1,0:T(8,128)(2,1)S(1)}, bf16[2,128,128]{2,1,0:T(8,128)(2,1)}, u32[]{:S(2)}) copy-start(bf16[2,128,128]{2,1,0:T(8,128)(2,1)} %ow_ref.3) | copy-start | bytes 196612
  66.3 41.3 %copy-start.6 = (bf16[2,128,128]{2,1,0:T(8,128)(2,1)S(1)}, bf16[2,128,128]{2,1,0:T(8,128)(2,1)}, u32[]{:S(2)}) copy-start(bf16[2,128,128]{2,1,0:T(8,128)(2,1)} %gw_ref.3) | copy-start | bytes 196612
  66.4 41.3 %copy-start.10 = (f32[2,128]{1,0:T(2,128)S(1)}, f32[2,128]{1,0:T(2,128)}, u32[]{:S(2)}) copy-start(f32[2,128]{1,0:T(2,128)} %bias_ref.3) | copy-start | bytes 3076
  66.4 41.3 %copy-start.11 = (f32[2,128]{1,0:T(2,128)S(1)}, f32[2,128]{1,0:T(2,128)}, u32[]{:S(2)}) copy-start(f32[2,128]{1,0:T(2,128)} %og_ref.3) | copy-start | bytes 3076
  66.4 41.3 %copy-start.12 = (f32[2,128]{1,0:T(2,128)S(1)}, f32[2,128]{1,0:T(2,128)}, u32[]{:S(2)}) copy-start(f32[2,128]{1,0:T(2,128)} %ob_ref.3) | copy-start | bytes 3076
  107.7 0.7 copy-start.8
  155.4 4.5 %collective-permute-start.1 = (bf16[16,16,16,128]{3,2,1,0:T(8,128)(2,1)S(1)}, bf16[16,16,16,128]{3,2,1,0:T(8,128)(2,1)S(1)}, u32[]{:S(2)}, u32[]{:S(2)}) collective-permute-start(bf16[16,16,16,128]{3,2,1,0:T(8,128)(2,1)S(1)} %bitcast.11), channel_id=1, source_target_pairs={{0,16},{16,0},{1,17},{17,1},{2,18},{18,2},{3,19},{19,3},{4,20},{20... | collective-permute-start | bytes 3145736 | tf_op jit(solution)/shard_map/ppermute | solution.py:185

commit v2 on v1

v2 whole, which is shorter than its diff:
```python
import jax
import jax.numpy as jnp
from jax import lax
from jax.experimental import pallas as pl
from jax.experimental.pallas import tpu as pltpu
from jax.sharding import Mesh
from jax.sharding import PartitionSpec as P

OUTGOING = ("zhi", "y", "zlo", "xlo")
INCOMING = ("y", "zlo", "xhi", "xlo")
EPS = 1e-05
F32 = jnp.float32
BF16 = jnp.bfloat16

OPERAND_STEP = 40
PRODUCT_STEP = 24
OPERAND_SCRATCH = ((128 * OPERAND_STEP, 128), F32)
PRODUCT_SCRATCH = ((128 * PRODUCT_STEP, 128), F32)


def _norm(values, gain, bias):
    center = values - jnp.mean(values, axis=0, keepdims=True)
    spread = jnp.mean(center * center, axis=0, keepdims=True)
    return (center * lax.rsqrt(spread + EPS) * gain + bias).astype(BF16)


def _column(ref, u):
    return jnp.broadcast_to(ref[u : u + 1, :], (128, 128)).T


def _project(cells, gain, bias, turned_w, turned_gate_w, scr, s):
    normed = _norm(cells.astype(F32), gain, bias)
    halves = jnp.dot(turned_w, normed, preferred_element_type=F32)
    left = jax.nn.sigmoid(halves[128:256]) * halves[:128]
    right = jax.nn.sigmoid(halves[384:]) * halves[256:384]
    scr[pl.ds(s, 128, stride=OPERAND_STEP), :] = left
    scr[pl.ds(16 + s, 128, stride=OPERAND_STEP), :] = right
    return jax.nn.sigmoid(jnp.dot(turned_gate_w, normed, preferred_element_type=F32))


def _put_operands(out_ref, scr):
    rows = scr[...].reshape(128, OPERAND_STEP, 128)[:, :32]
    out_ref[...] = rows.astype(BF16).reshape(4096, 128)


def _first_kernel(p_ref, gain_ref, bias_ref, w_ref, gw_ref, out_ref, gate_ref, turned_ref, scr):
    turned_w, turned_gate_w = w_ref[0].T, gw_ref[0].T
    gain, bias = _column(gain_ref, 0), _column(bias_ref, 0)
    for s in range(16):
        cells = jnp.concatenate([p_ref[s], p_ref[16 + s]], axis=0).T
        turned_ref[s] = cells
        gate_ref[s] = _project(cells, gain, bias, turned_w, turned_gate_w, scr, s)
    _put_operands(out_ref, scr)


def _load_products(one, two, scr):
    total = (one.astype(F32) + two.astype(F32)).reshape(128, 16, 128)
    for c in range(128):
        scr[c * PRODUCT_STEP : c * PRODUCT_STEP + 16, :] = total[c]


def _finished(scr, s, cells, gate, gain, bias, turned_w):
    mixed = _norm(scr[pl.ds(s, 128, stride=PRODUCT_STEP), :], gain, bias)
    projected = jnp.dot(turned_w, mixed, preferred_element_type=F32)
    return (cells.astype(F32) + gate * projected).astype(BF16)


def _middle_kernel(
    t_ref, p_ref, g_ref, og_ref, ob_ref, ow_ref, gain_ref, bias_ref, w_ref, gw_ref,
    mid_ref, out_ref, gate_ref, tri_scr, scr,
):
    _load_products(t_ref[:, 0], t_ref[:, 1], tri_scr)
    turned_w, turned_gate_w, turned_out_w = w_ref[1].T, gw_ref[1].T, ow_ref[0].T
    gain, bias = _column(gain_ref, 1), _column(bias_ref, 1)
    out_gain, out_bias = _column(og_ref, 0), _column(ob_ref, 0)
    for s in range(16):
        mid_ref[s] = _finished(
            tri_scr, s, p_ref[s], g_ref[s], out_gain, out_bias, turned_out_w
        )
    for s in range(16):
        gate_ref[s] = _project(mid_ref[s], gain, bias, turned_w, turned_gate_w, scr, s)
    _put_operands(out_ref, scr)


def _last_kernel(t_ref, p_ref, g_ref, og_ref, ob_ref, ow_ref, out_ref, tri_scr):
    _load_products(t_ref[0], t_ref[1], tri_scr)
    turned_w = ow_ref[1].T
    gain, bias = _column(og_ref, 1), _column(ob_ref, 1)
    for s in range(16):
        out = _finished(tri_scr, s, p_ref[s], g_ref[s], gain, bias, turned_w).T
        out_ref[s] = out[:64]
        out_ref[16 + s] = out[64:]


def _pair_up(one, two):
    low = jnp.concatenate([one[..., :64], two[..., :64]], axis=-1)
    high = jnp.concatenate([one[..., 64:], two[..., 64:]], axis=-1)
    return low, high


def _quarter(parts, q):
    return jnp.concatenate([part[..., 32 * q : 32 * q + 32] for part in parts], axis=-1)


def _put_products(out_ref, rows, tri):
    tri = tri.astype(BF16).reshape(-1, 2, 16, 1024)
    for pair in range(8):
        lanes = tri[..., pair * 128 : pair * 128 + 128]
        low, high = _pair_up(lanes[:, 0], lanes[:, 1])
        out_ref[rows, 2 * pair] = low
        out_ref[rows, 2 * pair + 1] = high


def _outgoing_kernel(core_ref, own_ref, other_ref, out_ref, l_scr, r_scr):
    core = core_ref[0]
    for pair in range(4):
        lanes = slice(pair * 128, pair * 128 + 128)
        left = _pair_up(own_ref[:, 2 * pair, 0], own_ref[:, 2 * pair + 1, 0])
        right = _pair_up(own_ref[:, 2 * pair, 1], own_ref[:, 2 * pair + 1, 1])
        away = _pair_up(other_ref[:, 2 * pair, 1], other_ref[:, 2 * pair + 1, 1])
        for b in range(2):
            l_scr[:, b, :, lanes] = left[b]
            r_scr[:, pl.ds(core, 1), b, :, lanes] = right[b][:, None]
            r_scr[:, pl.ds(1 - core, 1), b, :, lanes] = away[b][:, None]
    right = r_scr[...].reshape(1024, 512)
    for part in range(2):
        rows = slice(part * 8, part * 8 + 8)
        left = l_scr[rows].reshape(256, 512)
        tri = lax.dot_general(left, right, (((1,), (1,)), ((), ())), preferred_element_type=F32)
        _put_products(out_ref, rows, tri)


def _incoming_kernel(core_ref, own_ref, other_ref, out_ref, l_scr, r_scr):
    first = core_ref[0] == 0
    for at, ref in ((0, own_ref), (1, other_ref)):
        for zlo in range(4):
            parts = [ref[:, zlo * 4 + x, 0] for x in range(4)]
            lanes = slice(zlo * 128, zlo * 128 + 128)
            for b in range(2):
                l_scr[at, b, :, :, lanes] = jnp.where(
                    first, _quarter(parts, 2 * b), _quarter(parts, 2 * b + 1)
                )
        for pair in range(8):
            lanes = slice(pair * 128, pair * 128 + 128)
            right = _pair_up(ref[:, 2 * pair, 1], ref[:, 2 * pair + 1, 1])
            for b in range(2):
                r_scr[at, b, :, :, lanes] = right[b]
    right = r_scr[...].reshape(512, 1024)
    for part in range(2):
        left = l_scr[:, :, :, :, part * 256 : part * 256 + 256].reshape(512, 256)
        tri = lax.dot_general(left, right, (((0,), (0,)), ((), ())), preferred_element_type=F32)
        _put_products(out_ref, slice(part * 8, part * 8 + 8), tri)


def _call(kernel, outs, scratch, args, scalar=False, fetch=False):
    whole = pl.BlockSpec(memory_space=pltpu.VMEM)
    specs = [whole for _ in args]
    grid = ()
    if scalar:
        specs[0] = pl.BlockSpec(memory_space=pltpu.SMEM)
    if fetch:
        grid = (1,)
        specs = [pl.BlockSpec(arg.shape, lambda i, n=arg.ndim: (0,) * n) for arg in args]
    return pl.pallas_call(
        kernel,
        grid=grid,
        out_shape=[jax.ShapeDtypeStruct(shape, dtype) for shape, dtype in outs],
        in_specs=specs,
        out_specs=[whole for _ in outs],
        scratch_shapes=[pltpu.VMEM(shape, dtype) for shape, dtype in scratch],
        compiler_params=pltpu.CompilerParams(vmem_limit_bytes=(60 if fetch else 40) << 20),
    )(*args)


def _exchange(tiles, group):
    return lax.all_to_all(tiles, group, split_axis=0, concat_axis=0, tiled=True)


def _products(kernel, group, sources, scratch, tiles):
    own = _exchange(tiles.reshape(128, 32, 128), group).reshape(*sources, 2, 16, 128)
    other = lax.ppermute(own, "core", [(0, 1), (1, 0)])
    core = lax.axis_index("core").astype(jnp.int32).reshape(1)
    (out,) = _call(
        kernel, [((16, 16, 16, 128), BF16)], scratch, (core, own, other), scalar=True
    )
    return _exchange(out.reshape(256, 16, 128), ("zhi", "y", "zlo", "xhi", "xlo"))


def body(pair_rep, in_gain, in_bias, proj_w, gate_w, out_gain, out_bias, out_w):
    turned = (16, 128, 128)
    tiles, gate, cells = _call(
        _first_kernel,
        [((4096, 128), BF16), (turned, F32), (turned, BF16)],
        [OPERAND_SCRATCH],
        (pair_rep, in_gain, in_bias, proj_w, gate_w),
        fetch=True,
    )
    tri = _products(
        _outgoing_kernel,
        OUTGOING,
        (16, 8),
        [((16, 2, 16, 512), BF16), ((16, 2, 2, 16, 512), BF16)],
        tiles,
    ).reshape(64, 2, 2, 16, 128)
    middle, tiles, gate = _call(
        _middle_kernel,
        [(turned, BF16), ((4096, 128), BF16), (turned, F32)],
        [PRODUCT_SCRATCH, OPERAND_SCRATCH],
        (tri, cells, gate, out_gain, out_bias, out_w, in_gain, in_bias, proj_w, gate_w),
    )
    tri = _products(
        _incoming_kernel,
        INCOMING,
        (8, 16),
        [((2, 2, 8, 16, 512), BF16), ((2, 2, 8, 16, 1024), BF16)],
        tiles,
    ).reshape(2, 128, 16, 128)
    (out,) = _call(
        _last_kernel,
        [(pair_rep.shape, BF16)],
        [PRODUCT_SCRATCH],
        (tri, middle, gate, out_gain, out_bias, out_w),
    )
    return out


def solution(mesh):
    fine = Mesh(
        mesh.devices.reshape(2, 8, 2, 4, 2, 2), ("zhi", "y", "core", "zlo", "xhi", "xlo")
    )
    cells = P(("zhi", "y", "core"), ("zlo", "xhi", "xlo"), None)
    placed = (cells, P(), P(), P(), P(), P(), P(), P())
    return jax.shard_map(body, mesh=fine, in_specs=placed, out_specs=cells, check_vma=False)
```

time: 207 us -> 192 us (0.928)
  Pallas kernels: 16.7 us -> 10.8 us
  blocking collectives: 174 us -> 169 us
  local copies, waits for them, and re-layouts: 4.86 us -> 0.67 us
    pallas_call x5, Pallas kernels: 16.7 us -> 10.8 us  [_call(): pl.pallas_call(kernel, grid=grid, out_shape=[jax.ShapeDtypeStruct(shape,...]
    all_to_all x4, blocking collectives: 174 us -> 169 us  [_exchange(): return lax.all_to_all(tiles, group, split_axis=0, concat_axis=0, tiled=True)]
    unnamed x26 -> x18, local copies, waits for them, and re-layouts: 4.86 us -> 0.67 us
where the time goes in v2:
time: 192 us; the launch traced here: 190 us
  blocking collectives  169 us (88%)
  Pallas kernels  10.8 us (6%)
  waiting for transfers between devices  5.25 us (3%)
  starting transfers between devices  3.82 us (2%)
    all_to_all x4, blocking collectives, _exchange(): return lax.all_to_all(tiles, group, split_axis=0, concat_axis=0, tiled=True)  169 us
    pallas_call x5, Pallas kernels, _call(): pl.pallas_call(kernel, grid=grid, out_shape=[jax.ShapeDtypeStruct(shape,...  10.8 us
    ppermute x2, waiting for transfers between devices, _products(): other = lax.ppermute(own, 'core', [(0, 1), (1, 0)])  5.25 us
  transfers between devices with their start and end apart: 2, of which 2 were waited for; matrix products, arithmetic and copies ran while one was open for 0% of the time, Pallas kernels for 0%

profile of v2, /device:TPU:6, one launch (start us, length us, event | category | flops | bytes accessed | tf_op | source)
XLA Modules:
  0.0 189.7 jit_solution(8809611983101219068)
XLA Ops:
  0.0 4.0 %shard_map.82 = (bf16[4096,128]{1,0:T(8,128)(2,1)}, f32[16,128,128]{2,1,0:T(8,128)}, bf16[16,128,128]{2,1,0:T(8,128)(2,1)}) custom-call(bf16[32,64,128]{2,1,0:T(8,128)(2,1)} %p_ref.1, f32[2,128]{1,0:T(2,128)} %gain_ref.3, f32[2,128]{1,0:T(2,128)} %bias_ref.3, bf16[2,128,512]{2,1,0:T(8,128)(2,1)} %w_ref.3, bf16[2,128,128]{2,1,0:T(8,128)(2,1)} %gw_ref.3), custom_call_target="tpu_custom_call" | custom-call | tf_op jit(solution)/shard_map/pallas_call | solution.py:164
  4.0 49.0 %all_to_all.20 = bf16[128,32,128]{2,1,0:T(8,128)(2,1)S(1)} all-to-all(bf16[128,32,128]{2,1,0:T(8,128)(2,1)} %bitcast.18), channel_id=1, replica_groups=mesh['zhi'=2,'y'=8,'core'=2,'zlo'=4,'xhi'=2,'xlo'=2] {'zhi','y','zlo','x..., dimensions={0} | all-to-all | bytes 2097152 | tf_op jit(solution)/shard_map/all_to_all | solution.py:176
  52.9 1.9 %collective-permute-start = (bf16[16,8,2,16,128]{4,3,2,1,0:T(8,128)(2,1)S(1)}, bf16[16,8,2,16,128]{4,3,2,1,0:T(8,128)(2,1)S(1)}, u32[]{:S(2)}, u32[]{:S(2)}) collective-permute-start(bf16[16,8,2,16,128]{4,3,2,1,0:T(8,128)(2,1)S(1)} %bitcast.9), channel_id=1, source_target_pairs={{0,16},{16,0},{1,17},{17,1},{2,18},{18,2},{3,19},{19,3},{4,20},{20... | collective-permute-start | bytes 3145736 | tf_op jit(solution)/shard_map/ppermute | solution.py:181
  54.9 2.6 %collective-permute-done.other_ref = bf16[16,8,2,16,128]{4,3,2,1,0:T(8,128)(2,1)S(1)} collective-permute-done((bf16[16,8,2,16,128]{4,3,2,1,0:T(8,128)(2,1)S(1)}, bf16[16,8,2,16,128]{4,3,2,1,0:T(8,128)(2,1)S(1)}, u32[]{:S(2)}, u32[]{:S(2)}) %collective-permute-start) | collective-permute-done | bytes 1048608 | tf_op jit(solution)/shard_map/ppermute | solution.py:181
  57.5 1.2 shard_map.83
  58.7 0.0 copy-start
  58.7 0.0 copy-start.1
  58.7 0.0 copy-start.2
  58.7 0.0 copy-start.3
  58.7 0.0 copy-start.4
  58.7 0.0 copy-start.6
  58.7 0.0 copy-start.7
  58.7 0.0 copy-start.8
  58.8 40.8 %all_to_all.21 = bf16[256,16,128]{2,1,0:T(8,128)(2,1)S(1)} all-to-all(bf16[256,16,128]{2,1,0:T(8,128)(2,1)S(1)} %bitcast.15), channel_id=1, replica_groups=mesh['zhi'=2,'y'=8,'core'=2,'zlo'=4,'xhi'=2,'xlo'=2] {'zhi','y','zlo','x..., dimensions={0} | all-to-all | bytes 2097152 | tf_op jit(solution)/shard_map/all_to_all | solution.py:176
  99.5 0.0 copy-start.5
  99.5 0.0 copy-done
  99.5 0.0 copy-done.1
  99.5 0.0 copy-done.2
  99.5 0.0 copy-done.3
  99.5 0.0 copy-done.4
  99.6 0.0 copy-done.6
  99.6 0.0 copy-done.7
  99.6 0.0 copy-done.8
  99.6 0.6 copy-done.5
  100.2 2.0 %shard_map.84 = (bf16[16,128,128]{2,1,0:T(8,128)(2,1)S(1)}, bf16[4096,128]{1,0:T(8,128)(2,1)S(1)}, f32[16,128,128]{2,1,0:T(8,128)S(1)}) custom-call(bf16[64,2,2,16,128]{4,3,2,1,0:T(8,128)(2,1)S(1)} %bitcast.13, bf16[16,128,128]{2,1,0:T(8,128)(2,1)S(1)} %copy-done.2, f32[16,128,128]{2,1,0:T(8,128)S(1)} %copy-done.1, f32[2,128]{1,0:T(2,128)S(1)} %copy-done.7, ...), custom_call_target="tpu_custom_call" | custom-call | tf_op jit(solution)/shard_map/pallas_call | solution.py:164
  102.2 38.8 %all_to_all.22 = bf16[128,32,128]{2,1,0:T(8,128)(2,1)S(1)} all-to-all(bf16[128,32,128]{2,1,0:T(8,128)(2,1)S(1)} %bitcast.17), channel_id=1, replica_groups=mesh['zhi'=2,'y'=8,'core'=2,'zlo'=4,'xhi'=2,'xlo'=2] {'y','zlo','xhi','x..., dimensions={0} | all-to-all | bytes 2097152 | tf_op jit(solution)/shard_map/all_to_all | solution.py:176
  141.0 1.9 %collective-permute-start.1 = (bf16[8,16,2,16,128]{4,3,2,1,0:T(8,128)(2,1)S(1)}, bf16[8,16,2,16,128]{4,3,2,1,0:T(8,128)(2,1)S(1)}, u32[]{:S(2)}, u32[]{:S(2)}) collective-permute-start(bf16[8,16,2,16,128]{4,3,2,1,0:T(8,128)(2,1)S(1)} %bitcast.11), channel_id=1, source_target_pairs={{0,16},{16,0},{1,17},{17,1},{2,18},{18,2},{3,19},{19,3},{4,20},{20... | collective-permute-start | bytes 3145736 | tf_op jit(solution)/shard_map/ppermute | solution.py:181
  142.9 2.6 %collective-permute-done.1.other_ref = bf16[8,16,2,16,128]{4,3,2,1,0:T(8,128)(2,1)S(1)} collective-permute-done((bf16[8,16,2,16,128]{4,3,2,1,0:T(8,128)(2,1)S(1)}, bf16[8,16,2,16,128]{4,3,2,1,0:T(8,128)(2,1)S(1)}, u32[]{:S(2)}, u32[]{:S(2)}) %collective-permute-start.1) | collective-permute-done | bytes 1048608 | tf_op jit(solution)/shard_map/ppermute | solution.py:181
  145.6 2.0 %shard_map.85 = bf16[16,16,16,128]{3,2,1,0:T(8,128)(2,1)S(1)} custom-call(s32[1]{0:T(128)} %bitcast.core_ref, bf16[8,16,2,16,128]{4,3,2,1,0:T(8,128)(2,1)S(1)} %bitcast.12, bf16[8,16,2,16,128]{4,3,2,1,0:T(8,128)(2,1)S(1)} %collective-permute-done.1.other_ref), custom_call_target="tpu_custom_call" | custom-call | tf_op jit(solution)/shard_map/pallas_call | solution.py:164
  147.5 40.5 %all_to_all.23 = bf16[256,16,128]{2,1,0:T(8,128)(2,1)S(1)} all-to-all(bf16[256,16,128]{2,1,0:T(8,128)(2,1)S(1)} %bitcast.14), channel_id=1, replica_groups=mesh['zhi'=2,'y'=8,'core'=2,'zlo'=4,'xhi'=2,'xlo'=2] {'zhi','y','zlo','x..., dimensions={0} | all-to-all | bytes 2097152 | tf_op jit(solution)/shard_map/all_to_all | solution.py:176
  188.0 1.7 shard_map.86
Async XLA Ops:
  52.9 4.5 %collective-permute-start = (bf16[16,8,2,16,128]{4,3,2,1,0:T(8,128)(2,1)S(1)}, bf16[16,8,2,16,128]{4,3,2,1,0:T(8,128)(2,1)S(1)}, u32[]{:S(2)}, u32[]{:S(2)}) collective-permute-start(bf16[16,8,2,16,128]{4,3,2,1,0:T(8,128)(2,1)S(1)} %bitcast.9), channel_id=1, source_target_pairs={{0,16},{16,0},{1,17},{17,1},{2,18},{18,2},{3,19},{19,3},{4,20},{20... | collective-permute-start | bytes 3145736 | tf_op jit(solution)/shard_map/ppermute | solution.py:181
  58.7 40.9 %copy-start = (bf16[2,128,512]{2,1,0:T(8,128)(2,1)S(1)}, bf16[2,128,512]{2,1,0:T(8,128)(2,1)}, u32[]{:S(2)}) copy-start(bf16[2,128,512]{2,1,0:T(8,128)(2,1)} %w_ref.3) | copy-start | bytes 786436
  58.7 40.9 %copy-start.1 = (f32[16,128,128]{2,1,0:T(8,128)S(1)}, f32[16,128,128]{2,1,0:T(8,128)}, u32[]{:S(2)}) copy-start(f32[16,128,128]{2,1,0:T(8,128)} %get-tuple-element.13.g_ref) | copy-start | bytes 3145732
  58.7 40.8 %copy-start.2 = (bf16[16,128,128]{2,1,0:T(8,128)(2,1)S(1)}, bf16[16,128,128]{2,1,0:T(8,128)(2,1)}, u32[]{:S(2)}) copy-start(bf16[16,128,128]{2,1,0:T(8,128)(2,1)} %get-tuple-element.12.p_ref) | copy-start | bytes 1572868
  58.7 40.8 %copy-start.3 = (bf16[2,128,128]{2,1,0:T(8,128)(2,1)S(1)}, bf16[2,128,128]{2,1,0:T(8,128)(2,1)}, u32[]{:S(2)}) copy-start(bf16[2,128,128]{2,1,0:T(8,128)(2,1)} %ow_ref.3) | copy-start | bytes 196612
  58.7 40.8 %copy-start.4 = (bf16[2,128,128]{2,1,0:T(8,128)(2,1)S(1)}, bf16[2,128,128]{2,1,0:T(8,128)(2,1)}, u32[]{:S(2)}) copy-start(bf16[2,128,128]{2,1,0:T(8,128)(2,1)} %gw_ref.3) | copy-start | bytes 196612
  58.7 40.8 %copy-start.6 = (f32[2,128]{1,0:T(2,128)S(1)}, f32[2,128]{1,0:T(2,128)}, u32[]{:S(2)}) copy-start(f32[2,128]{1,0:T(2,128)} %bias_ref.3) | copy-start | bytes 3076
  58.7 40.8 %copy-start.7 = (f32[2,128]{1,0:T(2,128)S(1)}, f32[2,128]{1,0:T(2,128)}, u32[]{:S(2)}) copy-start(f32[2,128]{1,0:T(2,128)} %og_ref.3) | copy-start | bytes 3076
  58.7 40.8 %copy-start.8 = (f32[2,128]{1,0:T(2,128)S(1)}, f32[2,128]{1,0:T(2,128)}, u32[]{:S(2)}) copy-start(f32[2,128]{1,0:T(2,128)} %ob_ref.3) | copy-start | bytes 3076
  99.5 0.7 copy-start.5
  141.0 4.5 %collective-permute-start.1 = (bf16[8,16,2,16,128]{4,3,2,1,0:T(8,128)(2,1)S(1)}, bf16[8,16,2,16,128]{4,3,2,1,0:T(8,128)(2,1)S(1)}, u32[]{:S(2)}, u32[]{:S(2)}) collective-permute-start(bf16[8,16,2,16,128]{4,3,2,1,0:T(8,128)(2,1)S(1)} %bitcast.11), channel_id=1, source_target_pairs={{0,16},{16,0},{1,17},{17,1},{2,18},{18,2},{3,19},{19,3},{4,20},{20... | collective-permute-start | bytes 3145736 | tf_op jit(solution)/shard_map/ppermute | solution.py:181

commit v3 on v2

--- a/solution.py
+++ b/solution.py
@@ -1,3 +1,5 @@
+import functools
+
 import jax
 import jax.numpy as jnp
 from jax import lax
@@ -6,14 +8,15 @@
 from jax.sharding import Mesh
 from jax.sharding import PartitionSpec as P
 
-OUTGOING = ("zhi", "y", "zlo", "xlo")
-INCOMING = ("y", "zlo", "xhi", "xlo")
+OUTGOING = ("zhi", "yhi", "ylo", "zlo", "xlo")
+INCOMING = ("zhi", "ylo", "zlo", "xhi", "xlo")
 EPS = 1e-05
 F32 = jnp.float32
 BF16 = jnp.bfloat16
 
 OPERAND_STEP = 40
 PRODUCT_STEP = 24
+STEP_ROWS = 16
 OPERAND_SCRATCH = ((128 * OPERAND_STEP, 128), F32)
 PRODUCT_SCRATCH = ((128 * PRODUCT_STEP, 128), F32)
 
@@ -24,8 +27,8 @@
     return (center * lax.rsqrt(spread + EPS) * gain + bias).astype(BF16)
 
 
-def _column(ref, u):
-    return jnp.broadcast_to(ref[u : u + 1, :], (128, 128)).T
+def _column(row):
+    return jnp.broadcast_to(row, (128, 128)).T
 
 
 def _project(cells, gain, bias, turned_w, turned_gate_w, scr, s):
@@ -43,14 +46,27 @@
     out_ref[...] = rows.astype(BF16).reshape(4096, 128)
 
 
-def _first_kernel(p_ref, gain_ref, bias_ref, w_ref, gw_ref, out_ref, gate_ref, turned_ref, scr):
+def _first_kernel(
+    p_ref, gain_ref, bias_ref, w_ref, gw_ref, og_ref, ob_ref,
+    out_ref, gate_ref, turned_ref, columns_ref, scr,
+):
+    step = pl.program_id(0)
     turned_w, turned_gate_w = w_ref[0].T, gw_ref[0].T
-    gain, bias = _column(gain_ref, 0), _column(bias_ref, 0)
-    for s in range(16):
-        cells = jnp.concatenate([p_ref[s], p_ref[16 + s]], axis=0).T
-        turned_ref[s] = cells
-        gate_ref[s] = _project(cells, gain, bias, turned_w, turned_gate_w, scr, s)
-    _put_operands(out_ref, scr)
+    gain, bias = _column(gain_ref[:1]), _column(bias_ref[:1])
+    for at in range(STEP_ROWS):
+        cells = jnp.concatenate([p_ref[0, at], p_ref[1, at]], axis=0).T
+        turned_ref[at] = cells
+        s = step * STEP_ROWS + at
+        gate_ref[at] = _project(cells, gain, bias, turned_w, turned_gate_w, scr, s)
+
+    @pl.when(step == pl.num_programs(0) - 1)
+    def _():
+        _put_operands(out_ref, scr)
+        columns_ref[0] = _column(gain_ref[1:])
+        columns_ref[1] = _column(bias_ref[1:])
+        for u in range(2):
+            columns_ref[2 + 2 * u] = _column(og_ref[u : u + 1])
+            columns_ref[3 + 2 * u] = _column(ob_ref[u : u + 1])
 
 
 def _load_products(one, two, scr):
@@ -66,13 +82,13 @@
 
 
 def _middle_kernel(
-    t_ref, p_ref, g_ref, og_ref, ob_ref, ow_ref, gain_ref, bias_ref, w_ref, gw_ref,
+    t_ref, p_ref, g_ref, columns_ref, ow_ref, w_ref, gw_ref,
     mid_ref, out_ref, gate_ref, tri_scr, scr,
 ):
     _load_products(t_ref[:, 0], t_ref[:, 1], tri_scr)
     turned_w, turned_gate_w, turned_out_w = w_ref[1].T, gw_ref[1].T, ow_ref[0].T
-    gain, bias = _column(gain_ref, 1), _column(bias_ref, 1)
-    out_gain, out_bias = _column(og_ref, 0), _column(ob_ref, 0)
+    gain, bias = columns_ref[0], columns_ref[1]
+    out_gain, out_bias = columns_ref[2], columns_ref[3]
     for s in range(16):
         mid_ref[s] = _finished(
             tri_scr, s, p_ref[s], g_ref[s], out_gain, out_bias, turned_out_w
@@ -82,10 +98,10 @@
     _put_operands(out_ref, scr)
 
 
-def _last_kernel(t_ref, p_ref, g_ref, og_ref, ob_ref, ow_ref, out_ref, tri_scr):
-    _load_products(t_ref[0], t_ref[1], tri_scr)
+def _last_kernel(t_ref, p_ref, g_ref, columns_ref, ow_ref, out_ref, tri_scr):
+    _load_products(t_ref[:, 0], t_ref[:, 1], tri_scr)
     turned_w = ow_ref[1].T
-    gain, bias = _column(og_ref, 1), _column(ob_ref, 1)
+    gain, bias = columns_ref[4], columns_ref[5]
     for s in range(16):
         out = _finished(tri_scr, s, p_ref[s], g_ref[s], gain, bias, turned_w).T
         out_ref[s] = out[:64]
@@ -131,15 +147,17 @@
 
 
 def _incoming_kernel(core_ref, own_ref, other_ref, out_ref, l_scr, r_scr):
-    first = core_ref[0] == 0
+    def load_left(core):
+        for at, ref in ((0, own_ref), (1, other_ref)):
+            for zlo in range(4):
+                parts = [ref[:, zlo * 4 + x, 0] for x in range(4)]
+                lanes = slice(zlo * 128, zlo * 128 + 128)
+                for b in range(2):
+                    l_scr[at, b, :, :, lanes] = _quarter(parts, 2 * b + core)
+
+    for core in range(2):
+        pl.when(core_ref[0] == core)(functools.partial(load_left, core))
     for at, ref in ((0, own_ref), (1, other_ref)):
-        for zlo in range(4):
-            parts = [ref[:, zlo * 4 + x, 0] for x in range(4)]
-            lanes = slice(zlo * 128, zlo * 128 + 128)
-            for b in range(2):
-                l_scr[at, b, :, :, lanes] = jnp.where(
-                    first, _quarter(parts, 2 * b), _quarter(parts, 2 * b + 1)
-                )
         for pair in range(8):
             lanes = slice(pair * 128, pair * 128 + 128)
             right = _pair_up(ref[:, 2 * pair, 1], ref[:, 2 * pair + 1, 1])
@@ -152,24 +170,47 @@
         _put_products(out_ref, slice(part * 8, part * 8 + 8), tri)
 
 
-def _call(kernel, outs, scratch, args, scalar=False, fetch=False):
+def _call(kernel, outs, scratch, args, scalar=False):
     whole = pl.BlockSpec(memory_space=pltpu.VMEM)
     specs = [whole for _ in args]
-    grid = ()
     if scalar:
         specs[0] = pl.BlockSpec(memory_space=pltpu.SMEM)
-    if fetch:
-        grid = (1,)
-        specs = [pl.BlockSpec(arg.shape, lambda i, n=arg.ndim: (0,) * n) for arg in args]
     return pl.pallas_call(
         kernel,
-        grid=grid,
         out_shape=[jax.ShapeDtypeStruct(shape, dtype) for shape, dtype in outs],
         in_specs=specs,
         out_specs=[whole for _ in outs],
         scratch_shapes=[pltpu.VMEM(shape, dtype) for shape, dtype in scratch],
-        compiler_params=pltpu.CompilerParams(vmem_limit_bytes=(60 if fetch else 40) << 20),
+        compiler_params=pltpu.CompilerParams(vmem_limit_bytes=40 << 20),
     )(*args)
+
+
+def _first(pair_rep, *params):
+    def whole(shape):
+        return pl.BlockSpec(shape, lambda i: (0,) * len(shape))
+
+    def part(shape, at):
+        return pl.BlockSpec(shape, lambda i: tuple(i if d == at else 0 for d in range(len(shape))))
+
+    return pl.pallas_call(
+        _first_kernel,
+        grid=(16 // STEP_ROWS,),
+        out_shape=[
+            jax.ShapeDtypeStruct((4096, 128), BF16),
+            jax.ShapeDtypeStruct((16, 128, 128), F32),
+            jax.ShapeDtypeStruct((16, 128, 128), BF16),
+            jax.ShapeDtypeStruct((6, 128, 128), F32),
+        ],
+        in_specs=[part((2, STEP_ROWS, 64, 128), 1)] + [whole(arg.shape) for arg in params],
+        out_specs=[
+            whole((4096, 128)),
+            part((STEP_ROWS, 128, 128), 0),
+            part((STEP_ROWS, 128, 128), 0),
+            whole((6, 128, 128)),
+        ],
+        scratch_shapes=[pltpu.VMEM(*OPERAND_SCRATCH)],
+        compiler_params=pltpu.CompilerParams(vmem_limit_bytes=60 << 20),
+    )(pair_rep.reshape(2, 16, 64, 128), *params)
 
 
 def _exchange(tiles, group):
@@ -183,17 +224,13 @@
     (out,) = _call(
         kernel, [((16, 16, 16, 128), BF16)], scratch, (core, own, other), scalar=True
     )
-    return _exchange(out.reshape(256, 16, 128), ("zhi", "y", "zlo", "xhi", "xlo"))
+    return _exchange(out.reshape(256, 16, 128), ("zhi", "yhi", "ylo", "zlo", "xhi", "xlo"))
 
 
 def body(pair_rep, in_gain, in_bias, proj_w, gate_w, out_gain, out_bias, out_w):
     turned = (16, 128, 128)
-    tiles, gate, cells = _call(
-        _first_kernel,
-        [((4096, 128), BF16), (turned, F32), (turned, BF16)],
-        [OPERAND_SCRATCH],
-        (pair_rep, in_gain, in_bias, proj_w, gate_w),
-        fetch=True,
+    tiles, gate, cells, columns = _first(
+        pair_rep, in_gain, in_bias, proj_w, gate_w, out_gain, out_bias
     )
     tri = _products(
         _outgoing_kernel,
@@ -206,7 +243,7 @@
         _middle_kernel,
         [(turned, BF16), ((4096, 128), BF16), (turned, F32)],
         [PRODUCT_SCRATCH, OPERAND_SCRATCH],
-        (tri, cells, gate, out_gain, out_bias, out_w, in_gain, in_bias, proj_w, gate_w),
+        (tri, cells, gate, columns, out_w, proj_w, gate_w),
     )
     tri = _products(
         _incoming_kernel,
@@ -214,20 +251,21 @@
         (8, 16),
         [((2, 2, 8, 16, 512), BF16), ((2, 2, 8, 16, 1024), BF16)],
         tiles,
-    ).reshape(2, 128, 16, 128)
+    ).reshape(2, 2, 64, 16, 128)
     (out,) = _call(
         _last_kernel,
         [(pair_rep.shape, BF16)],
         [PRODUCT_SCRATCH],
-        (tri, middle, gate, out_gain, out_bias, out_w),
+        (tri, middle, gate, columns, out_w),
     )
     return out
 
 
 def solution(mesh):
     fine = Mesh(
-        mesh.devices.reshape(2, 8, 2, 4, 2, 2), ("zhi", "y", "core", "zlo", "xhi", "xlo")
-    )
-    cells = P(("zhi", "y", "core"), ("zlo", "xhi", "xlo"), None)
+        mesh.devices.reshape(2, 2, 4, 2, 4, 2, 2),
+        ("zhi", "yhi", "ylo", "core", "zlo", "xhi", "xlo"),
+    )
+    cells = P(("zhi", "yhi", "ylo", "core"), ("zlo", "xhi", "xlo"), None)
     placed = (cells, P(), P(), P(), P(), P(), P(), P())
     return jax.shard_map(body, mesh=fine, in_specs=placed, out_specs=cells, check_vma=False)

time: 192 us -> 190 us (0.990)
  no operation moved by 1% of the time
where the time goes in v3:
time: 190 us; the launch traced here: 188 us
  blocking collectives  168 us (88%)
  Pallas kernels  10.6 us (6%)
  waiting for transfers between devices  5.25 us (3%)
  starting transfers between devices  3.82 us (2%)
    all_to_all x4, blocking collectives, _exchange(): return lax.all_to_all(tiles, group, split_axis=0, concat_axis=0, tiled=True)  168 us
    pallas_call x4, Pallas kernels, _call(): pl.pallas_call(kernel, out_shape=[jax.ShapeDtypeStruct(shape, dtype) for...  6.4 us
    ppermute x2, waiting for transfers between devices, _products(): other = lax.ppermute(own, 'core', [(0, 1), (1, 0)])  5.25 us
    pallas_call x1, Pallas kernels, _first(): pl.pallas_call(_first_kernel, grid=(16 // STEP_ROWS,), out_shape=[jax.Sha...  4.16 us
    ppermute x2, starting transfers between devices, _products(): other = lax.ppermute(own, 'core', [(0, 1), (1, 0)])  3.82 us
  transfers between devices with their start and end apart: 2, of which 2 were waited for; matrix products, arithmetic and copies ran while one was open for 0% of the time, Pallas kernels for 0%

profile of v3, /device:TPU:6, one launch (start us, length us, event | category | flops | bytes accessed | tf_op | source)
XLA Modules:
  0.0 187.9 jit_solution(1838414922909537180)
XLA Ops:
  0.0 4.2 %shard_map.82 = (bf16[4096,128]{1,0:T(8,128)(2,1)}, f32[16,128,128]{2,1,0:T(8,128)}, bf16[16,128,128]{2,1,0:T(8,128)(2,1)}, f32[6,128,128]{2,1,0:T(8,128)}) custom-call(bf16[2,16,64,128]{3,2,1,0:T(8,128)(2,1)} %bitcast.20, f32[2,128]{1,0:T(2,128)} %gain_ref.1, f32[2,128]{1,0:T(2,128)} %bias_ref.1, bf16[2,128,512]{2,1,0:T(8,128)(2,1)} %w_ref.3, ...), custom_call_target="tpu_custom_call" | custom-call | tf_op jit(solution)/shard_map/pallas_call | solution.py:195
  4.2 49.0 %all_to_all.20 = bf16[128,32,128]{2,1,0:T(8,128)(2,1)S(1)} all-to-all(bf16[128,32,128]{2,1,0:T(8,128)(2,1)} %bitcast.19), channel_id=1, replica_groups=mesh['zhi'=2,'yhi'=2,'ylo'=4,'core'=2,'zlo'=4,'xhi'=2,'xlo'=2] {'zhi','y..., dimensions={0} | all-to-all | bytes 2097152 | tf_op jit(solution)/shard_map/all_to_all | solution.py:217
  53.1 1.9 %collective-permute-start = (bf16[16,8,2,16,128]{4,3,2,1,0:T(8,128)(2,1)S(1)}, bf16[16,8,2,16,128]{4,3,2,1,0:T(8,128)(2,1)S(1)}, u32[]{:S(2)}, u32[]{:S(2)}) collective-permute-start(bf16[16,8,2,16,128]{4,3,2,1,0:T(8,128)(2,1)S(1)} %bitcast.11), channel_id=1, source_target_pairs={{0,16},{16,0},{1,17},{17,1},{2,18},{18,2},{3,19},{19,3},{4,20},{20... | collective-permute-start | bytes 3145736 | tf_op jit(solution)/shard_map/ppermute | solution.py:222
  55.1 2.6 %collective-permute-done.other_ref = bf16[16,8,2,16,128]{4,3,2,1,0:T(8,128)(2,1)S(1)} collective-permute-done((bf16[16,8,2,16,128]{4,3,2,1,0:T(8,128)(2,1)S(1)}, bf16[16,8,2,16,128]{4,3,2,1,0:T(8,128)(2,1)S(1)}, u32[]{:S(2)}, u32[]{:S(2)}) %collective-permute-start) | collective-permute-done | bytes 1048608 | tf_op jit(solution)/shard_map/ppermute | solution.py:222
  57.7 0.0 copy-start.3
  57.7 1.2 shard_map.83
  58.9 0.0 copy-start
  58.9 0.0 copy-start.1
  58.9 0.0 copy-start.2
  58.9 0.0 copy-start.4
  58.9 0.0 copy-start.5
  58.9 40.8 %all_to_all.21 = bf16[256,16,128]{2,1,0:T(8,128)(2,1)S(1)} all-to-all(bf16[256,16,128]{2,1,0:T(8,128)(2,1)S(1)} %bitcast.17), channel_id=1, replica_groups=mesh['zhi'=2,'yhi'=2,'ylo'=4,'core'=2,'zlo'=4,'xhi'=2,'xlo'=2] {'zhi','y..., dimensions={0} | all-to-all | bytes 2097152 | tf_op jit(solution)/shard_map/all_to_all | solution.py:217
  99.7 0.0 copy-done.3
  99.7 0.0 copy-done
  99.7 0.0 copy-done.1
  99.7 0.0 copy-done.2
  99.7 0.0 copy-done.4
  99.7 0.0 copy-done.5
  99.7 2.0 %shard_map.84 = (bf16[16,128,128]{2,1,0:T(8,128)(2,1)S(1)}, bf16[4096,128]{1,0:T(8,128)(2,1)S(1)}, f32[16,128,128]{2,1,0:T(8,128)S(1)}) custom-call(bf16[64,2,2,16,128]{4,3,2,1,0:T(8,128)(2,1)S(1)} %bitcast.15, bf16[16,128,128]{2,1,0:T(8,128)(2,1)S(1)} %copy-done.3, f32[16,128,128]{2,1,0:T(8,128)S(1)} %copy-done.1, f32[6,128,128]{2,1,0:T(8,128)S(1)} %copy-done, ...), custom_call_target="tpu_custom_call" | custom-call | tf_op jit(solution)/shard_map/pallas_call | solution.py:178
  101.7 37.1 %all_to_all.22 = bf16[128,32,128]{2,1,0:T(8,128)(2,1)S(1)} all-to-all(bf16[128,32,128]{2,1,0:T(8,128)(2,1)S(1)} %bitcast.18), channel_id=1, replica_groups=mesh['zhi'=2,'yhi'=2,'ylo'=4,'core'=2,'zlo'=4,'xhi'=2,'xlo'=2] {'zhi','y..., dimensions={0} | all-to-all | bytes 2097152 | tf_op jit(solution)/shard_map/all_to_all | solution.py:217
  138.9 1.9 %collective-permute-start.1 = (bf16[8,16,2,16,128]{4,3,2,1,0:T(8,128)(2,1)S(1)}, bf16[8,16,2,16,128]{4,3,2,1,0:T(8,128)(2,1)S(1)}, u32[]{:S(2)}, u32[]{:S(2)}) collective-permute-start(bf16[8,16,2,16,128]{4,3,2,1,0:T(8,128)(2,1)S(1)} %bitcast.13), channel_id=1, source_target_pairs={{0,16},{16,0},{1,17},{17,1},{2,18},{18,2},{3,19},{19,3},{4,20},{20... | collective-permute-start | bytes 3145736 | tf_op jit(solution)/shard_map/ppermute | solution.py:222
  140.8 2.6 %collective-permute-done.1.other_ref = bf16[8,16,2,16,128]{4,3,2,1,0:T(8,128)(2,1)S(1)} collective-permute-done((bf16[8,16,2,16,128]{4,3,2,1,0:T(8,128)(2,1)S(1)}, bf16[8,16,2,16,128]{4,3,2,1,0:T(8,128)(2,1)S(1)}, u32[]{:S(2)}, u32[]{:S(2)}) %collective-permute-start.1) | collective-permute-done | bytes 1048608 | tf_op jit(solution)/shard_map/ppermute | solution.py:222
  143.4 1.6 shard_map.85
  145.0 41.2 %all_to_all.23 = bf16[256,16,128]{2,1,0:T(8,128)(2,1)S(1)} all-to-all(bf16[256,16,128]{2,1,0:T(8,128)(2,1)S(1)} %bitcast.16), channel_id=1, replica_groups=mesh['zhi'=2,'yhi'=2,'ylo'=4,'core'=2,'zlo'=4,'xhi'=2,'xlo'=2] {'zhi','y..., dimensions={0} | all-to-all | bytes 2097152 | tf_op jit(solution)/shard_map/all_to_all | solution.py:217
  186.2 1.7 shard_map.86
Async XLA Ops:
  53.1 4.5 %collective-permute-start = (bf16[16,8,2,16,128]{4,3,2,1,0:T(8,128)(2,1)S(1)}, bf16[16,8,2,16,128]{4,3,2,1,0:T(8,128)(2,1)S(1)}, u32[]{:S(2)}, u32[]{:S(2)}) collective-permute-start(bf16[16,8,2,16,128]{4,3,2,1,0:T(8,128)(2,1)S(1)} %bitcast.11), channel_id=1, source_target_pairs={{0,16},{16,0},{1,17},{17,1},{2,18},{18,2},{3,19},{19,3},{4,20},{20... | collective-permute-start | bytes 3145736 | tf_op jit(solution)/shard_map/ppermute | solution.py:222
  57.7 42.0 %copy-start.3 = (bf16[16,128,128]{2,1,0:T(8,128)(2,1)S(1)}, bf16[16,128,128]{2,1,0:T(8,128)(2,1)}, u32[]{:S(2)}) copy-start(bf16[16,128,128]{2,1,0:T(8,128)(2,1)} %get-tuple-element.13.p_ref) | copy-start | bytes 1572868
  58.9 40.8 %copy-start = (f32[6,128,128]{2,1,0:T(8,128)S(1)}, f32[6,128,128]{2,1,0:T(8,128)}, u32[]{:S(2)}) copy-start(f32[6,128,128]{2,1,0:T(8,128)} %get-tuple-element.15.columns_ref) | copy-start | bytes 1179652
  58.9 40.8 %copy-start.1 = (f32[16,128,128]{2,1,0:T(8,128)S(1)}, f32[16,128,128]{2,1,0:T(8,128)}, u32[]{:S(2)}) copy-start(f32[16,128,128]{2,1,0:T(8,128)} %get-tuple-element.14.g_ref) | copy-start | bytes 3145732
  58.9 40.8 %copy-start.2 = (bf16[2,128,512]{2,1,0:T(8,128)(2,1)S(1)}, bf16[2,128,512]{2,1,0:T(8,128)(2,1)}, u32[]{:S(2)}) copy-start(bf16[2,128,512]{2,1,0:T(8,128)(2,1)} %w_ref.3) | copy-start | bytes 786436
  58.9 40.8 %copy-start.4 = (bf16[2,128,128]{2,1,0:T(8,128)(2,1)S(1)}, bf16[2,128,128]{2,1,0:T(8,128)(2,1)}, u32[]{:S(2)}) copy-start(bf16[2,128,128]{2,1,0:T(8,128)(2,1)} %ow_ref.3) | copy-start | bytes 196612
  58.9 40.8 %copy-start.5 = (bf16[2,128,128]{2,1,0:T(8,128)(2,1)S(1)}, bf16[2,128,128]{2,1,0:T(8,128)(2,1)}, u32[]{:S(2)}) copy-start(bf16[2,128,128]{2,1,0:T(8,128)(2,1)} %gw_ref.3) | copy-start | bytes 196612
  138.9 4.5 %collective-permute-start.1 = (bf16[8,16,2,16,128]{4,3,2,1,0:T(8,128)(2,1)S(1)}, bf16[8,16,2,16,128]{4,3,2,1,0:T(8,128)(2,1)S(1)}, u32[]{:S(2)}, u32[]{:S(2)}) collective-permute-start(bf16[8,16,2,16,128]{4,3,2,1,0:T(8,128)(2,1)S(1)} %bitcast.13), channel_id=1, source_target_pairs={{0,16},{16,0},{1,17},{17,1},{2,18},{18,2},{3,19},{19,3},{4,20},{20... | collective-permute-start | bytes 3145736 | tf_op jit(solution)/shard_map/ppermute | solution.py:222

commit v4 on v3

--- a/solution.py
+++ b/solution.py
@@ -16,9 +16,8 @@
 
 OPERAND_STEP = 40
 PRODUCT_STEP = 24
-STEP_ROWS = 16
-OPERAND_SCRATCH = ((128 * OPERAND_STEP, 128), F32)
-PRODUCT_SCRATCH = ((128 * PRODUCT_STEP, 128), F32)
+OPERAND_SCRATCH = ((129 * OPERAND_STEP, 128), F32)
+PRODUCT_SCRATCH = ((129 * PRODUCT_STEP, 128), F32)
 
 
 def _norm(values, gain, bias):
@@ -29,6 +28,19 @@
 
 def _column(row):
     return jnp.broadcast_to(row, (128, 128)).T
+
+
+def _beside(one, two):
+    return jnp.concatenate([one, two], axis=1)
+
+
+def _twice(one):
+    return _beside(one, one)
+
+
+def _put_two(ref, s, value):
+    ref[s] = value[:, :128]
+    ref[s + 1] = value[:, 128:]
 
 
 def _project(cells, gain, bias, turned_w, turned_gate_w, scr, s):
@@ -36,13 +48,15 @@
     halves = jnp.dot(turned_w, normed, preferred_element_type=F32)
     left = jax.nn.sigmoid(halves[128:256]) * halves[:128]
     right = jax.nn.sigmoid(halves[384:]) * halves[256:384]
-    scr[pl.ds(s, 128, stride=OPERAND_STEP), :] = left
-    scr[pl.ds(16 + s, 128, stride=OPERAND_STEP), :] = right
+    for i in range(2):
+        lanes = slice(128 * i, 128 * i + 128)
+        scr[pl.ds(s + i, 128, stride=OPERAND_STEP), :] = left[:, lanes]
+        scr[pl.ds(16 + s + i, 128, stride=OPERAND_STEP), :] = right[:, lanes]
     return jax.nn.sigmoid(jnp.dot(turned_gate_w, normed, preferred_element_type=F32))
 
 
 def _put_operands(out_ref, scr):
-    rows = scr[...].reshape(128, OPERAND_STEP, 128)[:, :32]
+    rows = scr[: 128 * OPERAND_STEP].reshape(128, OPERAND_STEP, 128)[:, :32]
     out_ref[...] = rows.astype(BF16).reshape(4096, 128)
 
 
@@ -50,23 +64,22 @@
     p_ref, gain_ref, bias_ref, w_ref, gw_ref, og_ref, ob_ref,
     out_ref, gate_ref, turned_ref, columns_ref, scr,
 ):
-    step = pl.program_id(0)
     turned_w, turned_gate_w = w_ref[0].T, gw_ref[0].T
-    gain, bias = _column(gain_ref[:1]), _column(bias_ref[:1])
-    for at in range(STEP_ROWS):
-        cells = jnp.concatenate([p_ref[0, at], p_ref[1, at]], axis=0).T
-        turned_ref[at] = cells
-        s = step * STEP_ROWS + at
-        gate_ref[at] = _project(cells, gain, bias, turned_w, turned_gate_w, scr, s)
-
-    @pl.when(step == pl.num_programs(0) - 1)
-    def _():
-        _put_operands(out_ref, scr)
-        columns_ref[0] = _column(gain_ref[1:])
-        columns_ref[1] = _column(bias_ref[1:])
-        for u in range(2):
-            columns_ref[2 + 2 * u] = _column(og_ref[u : u + 1])
-            columns_ref[3 + 2 * u] = _column(ob_ref[u : u + 1])
+    gain, bias = _twice(_column(gain_ref[:1])), _twice(_column(bias_ref[:1]))
+    for s in range(0, 16, 2):
+        one = jnp.concatenate([p_ref[s], p_ref[16 + s]], axis=0).T
+        two = jnp.concatenate([p_ref[s + 1], p_ref[17 + s]], axis=0).T
+        turned_ref[s] = one
+        turned_ref[s + 1] = two
+        cells = _beside(one, two)
+        gate = _project(cells, gain, bias, turned_w, turned_gate_w, scr, s)
+        _put_two(gate_ref, s, gate)
+    _put_operands(out_ref, scr)
+    columns_ref[0] = _column(gain_ref[1:])
+    columns_ref[1] = _column(bias_ref[1:])
+    for u in range(2):
+        columns_ref[2 + 2 * u] = _column(og_ref[u : u + 1])
+        columns_ref[3 + 2 * u] = _column(ob_ref[u : u + 1])
 
 
 def _load_products(one, two, scr):
@@ -75,10 +88,14 @@
         scr[c * PRODUCT_STEP : c * PRODUCT_STEP + 16, :] = total[c]
 
 
-def _finished(scr, s, cells, gate, gain, bias, turned_w):
-    mixed = _norm(scr[pl.ds(s, 128, stride=PRODUCT_STEP), :], gain, bias)
+def _finished(scr, s, p_ref, g_ref, gain, bias, turned_w):
+    tri = _beside(
+        scr[pl.ds(s, 128, stride=PRODUCT_STEP), :], scr[pl.ds(s + 1, 128, stride=PRODUCT_STEP), :]
+    )
+    mixed = _norm(tri, gain, bias)
     projected = jnp.dot(turned_w, mixed, preferred_element_type=F32)
-    return (cells.astype(F32) + gate * projected).astype(BF16)
+    cells = _beside(p_ref[s], p_ref[s + 1]).astype(F32)
+    return (cells + _beside(g_ref[s], g_ref[s + 1]) * projected).astype(BF16)
 
 
 def _middle_kernel(
@@ -87,25 +104,27 @@
 ):
     _load_products(t_ref[:, 0], t_ref[:, 1], tri_scr)
     turned_w, turned_gate_w, turned_out_w = w_ref[1].T, gw_ref[1].T, ow_ref[0].T
-    gain, bias = columns_ref[0], columns_ref[1]
-    out_gain, out_bias = columns_ref[2], columns_ref[3]
-    for s in range(16):
-        mid_ref[s] = _finished(
-            tri_scr, s, p_ref[s], g_ref[s], out_gain, out_bias, turned_out_w
-        )
-    for s in range(16):
-        gate_ref[s] = _project(mid_ref[s], gain, bias, turned_w, turned_gate_w, scr, s)
+    gain, bias, out_gain, out_bias = (_twice(columns_ref[i]) for i in range(4))
+    for s in range(0, 16, 2):
+        mid = _finished(tri_scr, s, p_ref, g_ref, out_gain, out_bias, turned_out_w)
+        _put_two(mid_ref, s, mid)
+    for s in range(0, 16, 2):
+        cells = _beside(mid_ref[s], mid_ref[s + 1])
+        gate = _project(cells, gain, bias, turned_w, turned_gate_w, scr, s)
+        _put_two(gate_ref, s, gate)
     _put_operands(out_ref, scr)
 
 
 def _last_kernel(t_ref, p_ref, g_ref, columns_ref, ow_ref, out_ref, tri_scr):
     _load_products(t_ref[:, 0], t_ref[:, 1], tri_scr)
     turned_w = ow_ref[1].T
-    gain, bias = columns_ref[4], columns_ref[5]
-    for s in range(16):
-        out = _finished(tri_scr, s, p_ref[s], g_ref[s], gain, bias, turned_w).T
+    gain, bias = _twice(columns_ref[4]), _twice(columns_ref[5])
+    for s in range(0, 16, 2):
+        out = _finished(tri_scr, s, p_ref, g_ref, gain, bias, turned_w).T
         out_ref[s] = out[:64]
-        out_ref[16 + s] = out[64:]
+        out_ref[16 + s] = out[64:128]
+        out_ref[s + 1] = out[128:192]
+        out_ref[17 + s] = out[192:]
 
 
 def _pair_up(one, two):
@@ -185,32 +204,23 @@
     )(*args)
 
 
-def _first(pair_rep, *params):
+def _first(*args):
     def whole(shape):
         return pl.BlockSpec(shape, lambda i: (0,) * len(shape))
 
-    def part(shape, at):
-        return pl.BlockSpec(shape, lambda i: tuple(i if d == at else 0 for d in range(len(shape))))
-
+    in_specs = [whole(arg.shape) for arg in args]
+    in_specs[3] = pl.BlockSpec((1, 128, 512), lambda i: (0, 0, 0))
+    in_specs[4] = pl.BlockSpec((1, 128, 128), lambda i: (0, 0, 0))
+    outs = [((4096, 128), BF16), ((16, 128, 128), F32), ((16, 128, 128), BF16), ((6, 128, 128), F32)]
     return pl.pallas_call(
         _first_kernel,
-        grid=(16 // STEP_ROWS,),
-        out_shape=[
-            jax.ShapeDtypeStruct((4096, 128), BF16),
-            jax.ShapeDtypeStruct((16, 128, 128), F32),
-            jax.ShapeDtypeStruct((16, 128, 128), BF16),
-            jax.ShapeDtypeStruct((6, 128, 128), F32),
-        ],
-        in_specs=[part((2, STEP_ROWS, 64, 128), 1)] + [whole(arg.shape) for arg in params],
-        out_specs=[
-            whole((4096, 128)),
-            part((STEP_ROWS, 128, 128), 0),
-            part((STEP_ROWS, 128, 128), 0),
-            whole((6, 128, 128)),
-        ],
+        grid=(1,),
+        out_shape=[jax.ShapeDtypeStruct(shape, dtype) for shape, dtype in outs],
+        in_specs=in_specs,
+        out_specs=[whole(shape) for shape, _ in outs],
         scratch_shapes=[pltpu.VMEM(*OPERAND_SCRATCH)],
         compiler_params=pltpu.CompilerParams(vmem_limit_bytes=60 << 20),
-    )(pair_rep.reshape(2, 16, 64, 128), *params)
+    )(*args)
 
 
 def _exchange(tiles, group):

time: 190 us -> 190 us (level)
  no operation moved by 1% of the time
where the time goes in v4:
time: 190 us; the launch traced here: 187 us
  blocking collectives  168 us (88%)
  Pallas kernels  10.2 us (5%)
  waiting for transfers between devices  5.25 us (3%)
  starting transfers between devices  3.82 us (2%)
    all_to_all x4, blocking collectives, _exchange(): return lax.all_to_all(tiles, group, split_axis=0, concat_axis=0, tiled=True)  168 us
    pallas_call x4, Pallas kernels, _call(): pl.pallas_call(kernel, out_shape=[jax.ShapeDtypeStruct(shape, dtype) for...  6.24 us
    ppermute x2, waiting for transfers between devices, _products(): other = lax.ppermute(own, 'core', [(0, 1), (1, 0)])  5.25 us
    pallas_call x1, Pallas kernels, _first(): pl.pallas_call(_first_kernel, grid=(1,), out_shape=[jax.ShapeDtypeStruct(...  3.96 us
    ppermute x2, starting transfers between devices, _products(): other = lax.ppermute(own, 'core', [(0, 1), (1, 0)])  3.82 us
  transfers between devices with their start and end apart: 2, of which 2 were waited for; matrix products, arithmetic and copies ran while one was open for 0% of the time, Pallas kernels for 0%

profile of v4, /device:TPU:6, one launch (start us, length us, event | category | flops | bytes accessed | tf_op | source)
XLA Modules:
  0.0 187.5 jit_solution(4693011009624752353)
XLA Ops:
  0.0 4.0 %shard_map.82 = (bf16[4096,128]{1,0:T(8,128)(2,1)}, f32[16,128,128]{2,1,0:T(8,128)}, bf16[16,128,128]{2,1,0:T(8,128)(2,1)}, f32[6,128,128]{2,1,0:T(8,128)}) custom-call(bf16[32,64,128]{2,1,0:T(8,128)(2,1)} %p_ref.1, f32[2,128]{1,0:T(2,128)} %gain_ref.1, f32[2,128]{1,0:T(2,128)} %bias_ref.1, bf16[2,128,512]{2,1,0:T(8,128)(2,1)} %w_ref.3, ...), custom_call_target="tpu_custom_call" | custom-call | tf_op jit(solution)/shard_map/pallas_call | solution.py:215
  4.0 49.0 %all_to_all.20 = bf16[128,32,128]{2,1,0:T(8,128)(2,1)S(1)} all-to-all(bf16[128,32,128]{2,1,0:T(8,128)(2,1)} %bitcast.18), channel_id=1, replica_groups=mesh['zhi'=2,'yhi'=2,'ylo'=4,'core'=2,'zlo'=4,'xhi'=2,'xlo'=2] {'zhi','y..., dimensions={0} | all-to-all | bytes 2097152 | tf_op jit(solution)/shard_map/all_to_all | solution.py:227
  52.9 1.9 %collective-permute-start = (bf16[16,8,2,16,128]{4,3,2,1,0:T(8,128)(2,1)S(1)}, bf16[16,8,2,16,128]{4,3,2,1,0:T(8,128)(2,1)S(1)}, u32[]{:S(2)}, u32[]{:S(2)}) collective-permute-start(bf16[16,8,2,16,128]{4,3,2,1,0:T(8,128)(2,1)S(1)} %bitcast.10), channel_id=1, source_target_pairs={{0,16},{16,0},{1,17},{17,1},{2,18},{18,2},{3,19},{19,3},{4,20},{20... | collective-permute-start | bytes 3145736 | tf_op jit(solution)/shard_map/ppermute | solution.py:232
  54.8 2.6 %collective-permute-done.other_ref = bf16[16,8,2,16,128]{4,3,2,1,0:T(8,128)(2,1)S(1)} collective-permute-done((bf16[16,8,2,16,128]{4,3,2,1,0:T(8,128)(2,1)S(1)}, bf16[16,8,2,16,128]{4,3,2,1,0:T(8,128)(2,1)S(1)}, u32[]{:S(2)}, u32[]{:S(2)}) %collective-permute-start) | collective-permute-done | bytes 1048608 | tf_op jit(solution)/shard_map/ppermute | solution.py:232
  57.5 0.0 copy-start.3
  57.5 1.2 shard_map.83
  58.6 0.0 copy-start
  58.7 0.0 copy-start.1
  58.7 0.0 copy-start.2
  58.7 0.0 copy-start.4
  58.7 0.0 copy-start.5
  58.7 40.8 %all_to_all.21 = bf16[256,16,128]{2,1,0:T(8,128)(2,1)S(1)} all-to-all(bf16[256,16,128]{2,1,0:T(8,128)(2,1)S(1)} %bitcast.16), channel_id=1, replica_groups=mesh['zhi'=2,'yhi'=2,'ylo'=4,'core'=2,'zlo'=4,'xhi'=2,'xlo'=2] {'zhi','y..., dimensions={0} | all-to-all | bytes 2097152 | tf_op jit(solution)/shard_map/all_to_all | solution.py:227
  99.5 0.0 copy-done.3
  99.5 0.0 copy-done
  99.5 0.0 copy-done.1
  99.5 0.0 copy-done.2
  99.5 0.0 copy-done.4
  99.5 0.0 copy-done.5
  99.5 1.8 shard_map.84
  101.3 37.1 %all_to_all.22 = bf16[128,32,128]{2,1,0:T(8,128)(2,1)S(1)} all-to-all(bf16[128,32,128]{2,1,0:T(8,128)(2,1)S(1)} %bitcast.17), channel_id=1, replica_groups=mesh['zhi'=2,'yhi'=2,'ylo'=4,'core'=2,'zlo'=4,'xhi'=2,'xlo'=2] {'zhi','y..., dimensions={0} | all-to-all | bytes 2097152 | tf_op jit(solution)/shard_map/all_to_all | solution.py:227
  138.5 1.9 %collective-permute-start.1 = (bf16[8,16,2,16,128]{4,3,2,1,0:T(8,128)(2,1)S(1)}, bf16[8,16,2,16,128]{4,3,2,1,0:T(8,128)(2,1)S(1)}, u32[]{:S(2)}, u32[]{:S(2)}) collective-permute-start(bf16[8,16,2,16,128]{4,3,2,1,0:T(8,128)(2,1)S(1)} %bitcast.12), channel_id=1, source_target_pairs={{0,16},{16,0},{1,17},{17,1},{2,18},{18,2},{3,19},{19,3},{4,20},{20... | collective-permute-start | bytes 3145736 | tf_op jit(solution)/shard_map/ppermute | solution.py:232
  140.4 2.6 %collective-permute-done.1.other_ref = bf16[8,16,2,16,128]{4,3,2,1,0:T(8,128)(2,1)S(1)} collective-permute-done((bf16[8,16,2,16,128]{4,3,2,1,0:T(8,128)(2,1)S(1)}, bf16[8,16,2,16,128]{4,3,2,1,0:T(8,128)(2,1)S(1)}, u32[]{:S(2)}, u32[]{:S(2)}) %collective-permute-start.1) | collective-permute-done | bytes 1048608 | tf_op jit(solution)/shard_map/ppermute | solution.py:232
  143.0 1.6 shard_map.85
  144.6 41.2 %all_to_all.23 = bf16[256,16,128]{2,1,0:T(8,128)(2,1)S(1)} all-to-all(bf16[256,16,128]{2,1,0:T(8,128)(2,1)S(1)} %bitcast.15), channel_id=1, replica_groups=mesh['zhi'=2,'yhi'=2,'ylo'=4,'core'=2,'zlo'=4,'xhi'=2,'xlo'=2] {'zhi','y..., dimensions={0} | all-to-all | bytes 2097152 | tf_op jit(solution)/shard_map/all_to_all | solution.py:227
  185.8 1.7 shard_map.86
Async XLA Ops:
  52.9 4.5 %collective-permute-start = (bf16[16,8,2,16,128]{4,3,2,1,0:T(8,128)(2,1)S(1)}, bf16[16,8,2,16,128]{4,3,2,1,0:T(8,128)(2,1)S(1)}, u32[]{:S(2)}, u32[]{:S(2)}) collective-permute-start(bf16[16,8,2,16,128]{4,3,2,1,0:T(8,128)(2,1)S(1)} %bitcast.10), channel_id=1, source_target_pairs={{0,16},{16,0},{1,17},{17,1},{2,18},{18,2},{3,19},{19,3},{4,20},{20... | collective-permute-start | bytes 3145736 | tf_op jit(solution)/shard_map/ppermute | solution.py:232
  57.5 42.0 %copy-start.3 = (bf16[16,128,128]{2,1,0:T(8,128)(2,1)S(1)}, bf16[16,128,128]{2,1,0:T(8,128)(2,1)}, u32[]{:S(2)}) copy-start(bf16[16,128,128]{2,1,0:T(8,128)(2,1)} %get-tuple-element.13.p_ref) | copy-start | bytes 1572868
  58.6 40.8 %copy-start = (f32[6,128,128]{2,1,0:T(8,128)S(1)}, f32[6,128,128]{2,1,0:T(8,128)}, u32[]{:S(2)}) copy-start(f32[6,128,128]{2,1,0:T(8,128)} %get-tuple-element.15.columns_ref) | copy-start | bytes 1179652
  58.7 40.8 %copy-start.1 = (f32[16,128,128]{2,1,0:T(8,128)S(1)}, f32[16,128,128]{2,1,0:T(8,128)}, u32[]{:S(2)}) copy-start(f32[16,128,128]{2,1,0:T(8,128)} %get-tuple-element.14.g_ref) | copy-start | bytes 3145732
  58.7 40.8 %copy-start.2 = (bf16[2,128,512]{2,1,0:T(8,128)(2,1)S(1)}, bf16[2,128,512]{2,1,0:T(8,128)(2,1)}, u32[]{:S(2)}) copy-start(bf16[2,128,512]{2,1,0:T(8,128)(2,1)} %w_ref.3) | copy-start | bytes 786436
  58.7 40.8 %copy-start.4 = (bf16[2,128,128]{2,1,0:T(8,128)(2,1)S(1)}, bf16[2,128,128]{2,1,0:T(8,128)(2,1)}, u32[]{:S(2)}) copy-start(bf16[2,128,128]{2,1,0:T(8,128)(2,1)} %ow_ref.3) | copy-start | bytes 196612
  58.7 40.8 %copy-start.5 = (bf16[2,128,128]{2,1,0:T(8,128)(2,1)S(1)}, bf16[2,128,128]{2,1,0:T(8,128)(2,1)}, u32[]{:S(2)}) copy-start(bf16[2,128,128]{2,1,0:T(8,128)(2,1)} %gw_ref.3) | copy-start | bytes 196612
  138.5 4.5 %collective-permute-start.1 = (bf16[8,16,2,16,128]{4,3,2,1,0:T(8,128)(2,1)S(1)}, bf16[8,16,2,16,128]{4,3,2,1,0:T(8,128)(2,1)S(1)}, u32[]{:S(2)}, u32[]{:S(2)}) collective-permute-start(bf16[8,16,2,16,128]{4,3,2,1,0:T(8,128)(2,1)S(1)} %bitcast.12), channel_id=1, source_target_pairs={{0,16},{16,0},{1,17},{17,1},{2,18},{18,2},{3,19},{19,3},{4,20},{20... | collective-permute-start | bytes 3145736 | tf_op jit(solution)/shard_map/ppermute | solution.py:232

commit v5 on v4

--- a/solution.py
+++ b/solution.py
@@ -43,7 +43,7 @@
     ref[s + 1] = value[:, 128:]
 
 
-def _project(cells, gain, bias, turned_w, turned_gate_w, scr, s):
+def _project(cells, gain, bias, turned_w, scr, s):
     normed = _norm(cells.astype(F32), gain, bias)
     halves = jnp.dot(turned_w, normed, preferred_element_type=F32)
     left = jax.nn.sigmoid(halves[128:256]) * halves[:128]
@@ -52,6 +52,10 @@
         lanes = slice(128 * i, 128 * i + 128)
         scr[pl.ds(s + i, 128, stride=OPERAND_STEP), :] = left[:, lanes]
         scr[pl.ds(16 + s + i, 128, stride=OPERAND_STEP), :] = right[:, lanes]
+
+
+def _gate(cells, gain, bias, turned_gate_w):
+    normed = _norm(cells.astype(F32), gain, bias)
     return jax.nn.sigmoid(jnp.dot(turned_gate_w, normed, preferred_element_type=F32))
 
 
@@ -60,21 +64,28 @@
     out_ref[...] = rows.astype(BF16).reshape(4096, 128)
 
 
-def _first_kernel(
-    p_ref, gain_ref, bias_ref, w_ref, gw_ref, og_ref, ob_ref,
-    out_ref, gate_ref, turned_ref, columns_ref, scr,
+def _turned_rows(p_ref, s):
+    return jnp.concatenate([p_ref[s], p_ref[16 + s]], axis=0).T
+
+
+def _first_kernel(p_ref, gain_ref, bias_ref, w_ref, out_ref, scr):
+    turned_w = w_ref[0].T
+    gain, bias = _twice(_column(gain_ref[:1])), _twice(_column(bias_ref[:1]))
+    for s in range(0, 16, 2):
+        cells = _beside(_turned_rows(p_ref, s), _turned_rows(p_ref, s + 1))
+        _project(cells, gain, bias, turned_w, scr, s)
+    _put_operands(out_ref, scr)
+
+
+def _first_gate_kernel(
+    p_ref, gain_ref, bias_ref, gw_ref, og_ref, ob_ref, gate_ref, turned_ref, columns_ref
 ):
-    turned_w, turned_gate_w = w_ref[0].T, gw_ref[0].T
+    turned_gate_w = gw_ref[0].T
     gain, bias = _twice(_column(gain_ref[:1])), _twice(_column(bias_ref[:1]))
     for s in range(0, 16, 2):
-        one = jnp.concatenate([p_ref[s], p_ref[16 + s]], axis=0).T
-        two = jnp.concatenate([p_ref[s + 1], p_ref[17 + s]], axis=0).T
-        turned_ref[s] = one
-        turned_ref[s + 1] = two
-        cells = _beside(one, two)
-        gate = _project(cells, gain, bias, turned_w, turned_gate_w, scr, s)
-        _put_two(gate_ref, s, gate)
-    _put_operands(out_ref, scr)
+        cells = _beside(_turned_rows(p_ref, s), _turned_rows(p_ref, s + 1))
+        _put_two(turned_ref, s, cells)
+        _put_two(gate_ref, s, _gate(cells, gain, bias, turned_gate_w))
     columns_ref[0] = _column(gain_ref[1:])
     columns_ref[1] = _column(bias_ref[1:])
     for u in range(2):
@@ -82,6 +93,14 @@
         columns_ref[3 + 2 * u] = _column(ob_ref[u : u + 1])
 
 
+def _middle_gate_kernel(p_ref, columns_ref, gw_ref, gate_ref):
+    turned_gate_w = gw_ref[1].T
+    gain, bias = (_twice(columns_ref[i]) for i in range(2))
+    for s in range(0, 16, 2):
+        cells = _beside(p_ref[s], p_ref[s + 1])
+        _put_two(gate_ref, s, _gate(cells, gain, bias, turned_gate_w))
+
+
 def _load_products(one, two, scr):
     total = (one.astype(F32) + two.astype(F32)).reshape(128, 16, 128)
     for c in range(128):
@@ -99,19 +118,16 @@
 
 
 def _middle_kernel(
-    t_ref, p_ref, g_ref, columns_ref, ow_ref, w_ref, gw_ref,
-    mid_ref, out_ref, gate_ref, tri_scr, scr,
+    t_ref, p_ref, g_ref, columns_ref, ow_ref, w_ref, mid_ref, out_ref, tri_scr, scr
 ):
     _load_products(t_ref[:, 0], t_ref[:, 1], tri_scr)
-    turned_w, turned_gate_w, turned_out_w = w_ref[1].T, gw_ref[1].T, ow_ref[0].T
+    turned_w, turned_out_w = w_ref[1].T, ow_ref[0].T
     gain, bias, out_gain, out_bias = (_twice(columns_ref[i]) for i in range(4))
     for s in range(0, 16, 2):
         mid = _finished(tri_scr, s, p_ref, g_ref, out_gain, out_bias, turned_out_w)
         _put_two(mid_ref, s, mid)
     for s in range(0, 16, 2):
-        cells = _beside(mid_ref[s], mid_ref[s + 1])
-        gate = _project(cells, gain, bias, turned_w, turned_gate_w, scr, s)
-        _put_two(gate_ref, s, gate)
+        _project(_beside(mid_ref[s], mid_ref[s + 1]), gain, bias, turned_w, scr, s)
     _put_operands(out_ref, scr)
 
 
@@ -201,6 +217,7 @@
         out_specs=[whole for _ in outs],
         scratch_shapes=[pltpu.VMEM(shape, dtype) for shape, dtype in scratch],
         compiler_params=pltpu.CompilerParams(vmem_limit_bytes=40 << 20),
+        cost_estimate=pl.CostEstimate(flops=1 << 28, bytes_accessed=4 << 20, transcendentals=0),
     )(*args)
 
 
@@ -210,14 +227,12 @@
 
     in_specs = [whole(arg.shape) for arg in args]
     in_specs[3] = pl.BlockSpec((1, 128, 512), lambda i: (0, 0, 0))
-    in_specs[4] = pl.BlockSpec((1, 128, 128), lambda i: (0, 0, 0))
-    outs = [((4096, 128), BF16), ((16, 128, 128), F32), ((16, 128, 128), BF16), ((6, 128, 128), F32)]
     return pl.pallas_call(
         _first_kernel,
         grid=(1,),
-        out_shape=[jax.ShapeDtypeStruct(shape, dtype) for shape, dtype in outs],
+        out_shape=jax.ShapeDtypeStruct((4096, 128), BF16),
         in_specs=in_specs,
-        out_specs=[whole(shape) for shape, _ in outs],
+        out_specs=whole((4096, 128)),
         scratch_shapes=[pltpu.VMEM(*OPERAND_SCRATCH)],
         compiler_params=pltpu.CompilerParams(vmem_limit_bytes=60 << 20),
     )(*args)
@@ -239,8 +254,13 @@
 
 def body(pair_rep, in_gain, in_bias, proj_w, gate_w, out_gain, out_bias, out_w):
     turned = (16, 128, 128)
-    tiles, gate, cells, columns = _first(
-        pair_rep, in_gain, in_bias, proj_w, gate_w, out_gain, out_bias
+    tiles = _first(pair_rep, in_gain, in_bias, proj_w)
+    tiles, again = lax.optimization_barrier((tiles, pair_rep))
+    gate, cells, columns = _call(
+        _first_gate_kernel,
+        [(turned, F32), (turned, BF16), ((6, 128, 128), F32)],
+        [],
+        (again, in_gain, in_bias, gate_w, out_gain, out_bias),
     )
     tri = _products(
         _outgoing_kernel,
@@ -249,12 +269,13 @@
         [((16, 2, 16, 512), BF16), ((16, 2, 2, 16, 512), BF16)],
         tiles,
     ).reshape(64, 2, 2, 16, 128)
-    middle, tiles, gate = _call(
+    middle, tiles = _call(
         _middle_kernel,
-        [(turned, BF16), ((4096, 128), BF16), (turned, F32)],
+        [(turned, BF16), ((4096, 128), BF16)],
         [PRODUCT_SCRATCH, OPERAND_SCRATCH],
-        (tri, cells, gate, columns, out_w, proj_w, gate_w),
-    )
+        (tri, cells, gate, columns, out_w, proj_w),
+    )
+    (gate,) = _call(_middle_gate_kernel, [(turned, F32)], [], (middle, columns, gate_w))
     tri = _products(
         _incoming_kernel,
         INCOMING,

time: 190 us -> 193 us (1.016)
  blocking collectives: 168 us -> 86.1 us
  waiting for transfers between devices: 5.25 us -> 63.8 us
  starting transfers between devices: 3.82 us -> 24.6 us
  local copies, waits for them, and re-layouts: 0.03 us -> 2.9 us
  Pallas kernels: 10.2 us -> 12.6 us
    all_to_all x4 -> x2, blocking collectives: 168 us -> 86.1 us  [_exchange(): return lax.all_to_all(tiles, group, split_axis=0, concat_axis=0, tiled=True)]
    all_to_all x0 -> x2, waiting for transfers between devices: none -> 58.6 us  [_exchange(): return lax.all_to_all(tiles, group, split_axis=0, concat_axis=0, tiled=True)]
    all_to_all x0 -> x2, starting transfers between devices: none -> 20.8 us  [_exchange(): return lax.all_to_all(tiles, group, split_axis=0, concat_axis=0, tiled=True)]
    pallas_call x4 -> x6, Pallas kernels: 6.24 us -> 9.44 us  [_call(): pl.pallas_call(kernel, out_shape=[jax.ShapeDtypeStruct(shape, dtype) for...]
    unnamed x12 -> x20, local copies, waits for them, and re-layouts: 0.03 us -> 2.9 us
  transfers between devices with their start and end apart: 2 -> 4, of which waited for: 2 -> 4; matrix products, arithmetic and copies ran while one was open for 0% -> 0% of each run, Pallas kernels for 0% -> 1%
where the time goes in v5:
time: 193 us; the launch traced here: 190 us
  blocking collectives  86.1 us (45%)
  waiting for transfers between devices  63.8 us (33%)
  starting transfers between devices  24.6 us (13%)
  Pallas kernels  12.6 us (7%)
  local copies, waits for them, and re-layouts  2.9 us (2%)
    all_to_all x2, blocking collectives, _exchange(): return lax.all_to_all(tiles, group, split_axis=0, concat_axis=0, tiled=True)  86.1 us
    all_to_all x2, waiting for transfers between devices, _exchange(): return lax.all_to_all(tiles, group, split_axis=0, concat_axis=0, tiled=True)  58.6 us
    all_to_all x2, starting transfers between devices, _exchange(): return lax.all_to_all(tiles, group, split_axis=0, concat_axis=0, tiled=True)  20.8 us
    pallas_call x6, Pallas kernels, _call(): pl.pallas_call(kernel, out_shape=[jax.ShapeDtypeStruct(shape, dtype) for...  9.44 us
    ppermute x2, waiting for transfers between devices, _products(): other = lax.ppermute(own, 'core', [(0, 1), (1, 0)])  5.25 us
  transfers between devices with their start and end apart: 4, of which 4 were waited for; matrix products, arithmetic and copies ran while one was open for 0% of the time, Pallas kernels for 1%

profile of v5, /device:TPU:6, one launch (start us, length us, event | category | flops | bytes accessed | tf_op | source)
XLA Modules:
  0.0 190.2 jit_solution(1523990577426824752)
XLA Ops:
  0.0 3.2 %shard_map.82 = bf16[4096,128]{1,0:T(8,128)(2,1)} custom-call(bf16[32,64,128]{2,1,0:T(8,128)(2,1)} %p_ref.2, f32[2,128]{1,0:T(2,128)} %gain_ref.3, f32[2,128]{1,0:T(2,128)} %bias_ref.3, bf16[2,128,512]{2,1,0:T(8,128)(2,1)} %w_ref.3), custom_call_target="tpu_custom_call" | custom-call | tf_op jit(solution)/shard_map/pallas_call | solution.py:230
  3.2 49.0 %all_to_all.20 = bf16[128,32,128]{2,1,0:T(8,128)(2,1)S(1)} all-to-all(bf16[128,32,128]{2,1,0:T(8,128)(2,1)} %bitcast.16), channel_id=1, replica_groups=mesh['zhi'=2,'yhi'=2,'ylo'=4,'core'=2,'zlo'=4,'xhi'=2,'xlo'=2] {'zhi','y..., dimensions={0} | all-to-all | bytes 2097152 | tf_op jit(solution)/shard_map/all_to_all | solution.py:242
  52.2 1.9 %collective-permute-start = (bf16[16,8,2,16,128]{4,3,2,1,0:T(8,128)(2,1)S(1)}, bf16[16,8,2,16,128]{4,3,2,1,0:T(8,128)(2,1)S(1)}, u32[]{:S(2)}, u32[]{:S(2)}) collective-permute-start(bf16[16,8,2,16,128]{4,3,2,1,0:T(8,128)(2,1)S(1)} %bitcast.11), channel_id=1, source_target_pairs={{0,16},{16,0},{1,17},{17,1},{2,18},{18,2},{3,19},{19,3},{4,20},{20... | collective-permute-start | bytes 3145736 | tf_op jit(solution)/shard_map/ppermute | solution.py:247
  54.1 2.6 %collective-permute-done.other_ref = bf16[16,8,2,16,128]{4,3,2,1,0:T(8,128)(2,1)S(1)} collective-permute-done((bf16[16,8,2,16,128]{4,3,2,1,0:T(8,128)(2,1)S(1)}, bf16[16,8,2,16,128]{4,3,2,1,0:T(8,128)(2,1)S(1)}, u32[]{:S(2)}, u32[]{:S(2)}) %collective-permute-start) | collective-permute-done | bytes 1048608 | tf_op jit(solution)/shard_map/ppermute | solution.py:247
  56.7 2.2 %shard_map.83 = bf16[16,16,16,128]{3,2,1,0:T(8,128)(2,1)} custom-call(s32[1]{0:T(128)} %bitcast.core_ref, bf16[16,8,2,16,128]{4,3,2,1,0:T(8,128)(2,1)S(1)} %bitcast.12, bf16[16,8,2,16,128]{4,3,2,1,0:T(8,128)(2,1)S(1)} %collective-permute-done.other_ref), custom_call_target="tpu_custom_call" | custom-call | flops 268435456 | bytes 4194304 | tf_op jit(solution)/shard_map/pallas_call | solution.py:213
  58.9 0.0 copy-start.5
  58.9 0.0 copy-start.6
  58.9 0.0 copy-start.9
  58.9 10.3 %all-to-all-start.1 = ((bf16[256,16,128]{2,1,0:T(8,128)(2,1)}), bf16[256,16,128]{2,1,0:T(8,128)(2,1)S(1)}, u32[]{:S(2)}, u32[]{:S(2)}) async-start(bf16[256,16,128]{2,1,0:T(8,128)(2,1)} %bitcast.3), calls=%async_computation.1 | async-start | bytes 2097152 | tf_op jit(solution)/shard_map/all_to_all | solution.py:242
  69.2 0.0 copy-done.5
  69.2 0.0 copy-done.6
  69.2 0.0 copy-done.7
  69.2 0.0 copy-done.8
  69.2 0.0 copy-done.9
  69.2 0.0 copy-start.3
  69.3 1.0 copy-done.3
  70.3 0.7 shard_map.84
  71.0 0.0 copy-start.1
  71.0 0.8 copy-done.1
  71.8 28.1 %all-to-all-done.1 = bf16[256,16,128]{2,1,0:T(8,128)(2,1)S(1)} async-done(((bf16[256,16,128]{2,1,0:T(8,128)(2,1)}), bf16[256,16,128]{2,1,0:T(8,128)(2,1)S(1)}, u32[]{:S(2)}, u32[]{:S(2)}) %all-to-all-start.1) | async-done | bytes 1048608 | tf_op jit(solution)/shard_map/all_to_all | solution.py:242
  99.9 0.0 copy-done
  99.9 0.0 copy-done.4
  99.9 1.0 copy-done.2
  100.9 1.8 shard_map.85
  102.7 37.1 %all_to_all.21 = bf16[128,32,128]{2,1,0:T(8,128)(2,1)S(1)} all-to-all(bf16[128,32,128]{2,1,0:T(8,128)(2,1)S(1)} %bitcast.15), channel_id=1, replica_groups=mesh['zhi'=2,'yhi'=2,'ylo'=4,'core'=2,'zlo'=4,'xhi'=2,'xlo'=2] {'zhi','y..., dimensions={0} | all-to-all | bytes 2097152 | tf_op jit(solution)/shard_map/all_to_all | solution.py:242
  139.9 1.9 %collective-permute-start.1 = (bf16[8,16,2,16,128]{4,3,2,1,0:T(8,128)(2,1)S(1)}, bf16[8,16,2,16,128]{4,3,2,1,0:T(8,128)(2,1)S(1)}, u32[]{:S(2)}, u32[]{:S(2)}) collective-permute-start(bf16[8,16,2,16,128]{4,3,2,1,0:T(8,128)(2,1)S(1)} %bitcast.13), channel_id=1, source_target_pairs={{0,16},{16,0},{1,17},{17,1},{2,18},{18,2},{3,19},{19,3},{4,20},{20... | collective-permute-start | bytes 3145736 | tf_op jit(solution)/shard_map/ppermute | solution.py:247
  141.8 2.6 %collective-permute-done.1.other_ref = bf16[8,16,2,16,128]{4,3,2,1,0:T(8,128)(2,1)S(1)} collective-permute-done((bf16[8,16,2,16,128]{4,3,2,1,0:T(8,128)(2,1)S(1)}, bf16[8,16,2,16,128]{4,3,2,1,0:T(8,128)(2,1)S(1)}, u32[]{:S(2)}, u32[]{:S(2)}) %collective-permute-start.1) | collective-permute-done | bytes 1048608 | tf_op jit(solution)/shard_map/ppermute | solution.py:247
  144.4 2.5 %shard_map.86 = bf16[16,16,16,128]{3,2,1,0:T(8,128)(2,1)} custom-call(s32[1]{0:T(128)} %bitcast.core_ref, bf16[8,16,2,16,128]{4,3,2,1,0:T(8,128)(2,1)S(1)} %bitcast.14, bf16[8,16,2,16,128]{4,3,2,1,0:T(8,128)(2,1)S(1)} %collective-permute-done.1.other_ref), custom_call_target="tpu_custom_call" | custom-call | flops 268435456 | bytes 4194304 | tf_op jit(solution)/shard_map/pallas_call | solution.py:213
  147.0 10.5 %all-to-all-start.3 = ((bf16[256,16,128]{2,1,0:T(8,128)(2,1)}), bf16[256,16,128]{2,1,0:T(8,128)(2,1)S(1)}, u32[]{:S(2)}, u32[]{:S(2)}) async-start(bf16[256,16,128]{2,1,0:T(8,128)(2,1)} %bitcast.7), calls=%async_computation.3 | async-start | bytes 2097152 | tf_op jit(solution)/shard_map/all_to_all | solution.py:242
  157.5 0.6 shard_map.87.g_ref
  158.1 30.5 %all-to-all-done.3 = bf16[256,16,128]{2,1,0:T(8,128)(2,1)S(1)} async-done(((bf16[256,16,128]{2,1,0:T(8,128)(2,1)}), bf16[256,16,128]{2,1,0:T(8,128)(2,1)S(1)}, u32[]{:S(2)}, u32[]{:S(2)}) %all-to-all-start.3) | async-done | bytes 1048608 | tf_op jit(solution)/shard_map/all_to_all | solution.py:242
  188.5 1.7 shard_map.88
  (5 shorter events, 0.0 us)
Async XLA Ops:
  52.2 4.5 %collective-permute-start = (bf16[16,8,2,16,128]{4,3,2,1,0:T(8,128)(2,1)S(1)}, bf16[16,8,2,16,128]{4,3,2,1,0:T(8,128)(2,1)S(1)}, u32[]{:S(2)}, u32[]{:S(2)}) collective-permute-start(bf16[16,8,2,16,128]{4,3,2,1,0:T(8,128)(2,1)S(1)} %bitcast.11), channel_id=1, source_target_pairs={{0,16},{16,0},{1,17},{17,1},{2,18},{18,2},{3,19},{19,3},{4,20},{20... | collective-permute-start | bytes 3145736 | tf_op jit(solution)/shard_map/ppermute | solution.py:247
  58.9 10.3 %copy-start.5 = (bf16[2,128,128]{2,1,0:T(8,128)(2,1)S(1)}, bf16[2,128,128]{2,1,0:T(8,128)(2,1)}, u32[]{:S(2)}) copy-start(bf16[2,128,128]{2,1,0:T(8,128)(2,1)} %gw_ref.3) | copy-start | bytes 196612
  58.9 10.3 %copy-start.6 = (f32[2,128]{1,0:T(2,128)S(1)}, f32[2,128]{1,0:T(2,128)}, u32[]{:S(2)}) copy-start(f32[2,128]{1,0:T(2,128)} %gain_ref.3) | copy-start | bytes 3076
  58.9 10.4 %copy-start.7 = (f32[2,128]{1,0:T(2,128)S(1)}, f32[2,128]{1,0:T(2,128)}, u32[]{:S(2)}) copy-start(f32[2,128]{1,0:T(2,128)} %bias_ref.3) | copy-start | bytes 3076
  58.9 10.4 %copy-start.8 = (f32[2,128]{1,0:T(2,128)S(1)}, f32[2,128]{1,0:T(2,128)}, u32[]{:S(2)}) copy-start(f32[2,128]{1,0:T(2,128)} %og_ref.1) | copy-start | bytes 3076
  58.9 10.4 %copy-start.9 = (f32[2,128]{1,0:T(2,128)S(1)}, f32[2,128]{1,0:T(2,128)}, u32[]{:S(2)}) copy-start(f32[2,128]{1,0:T(2,128)} %ob_ref.1) | copy-start | bytes 3076
  58.9 41.0 %all-to-all-start.1 = ((bf16[256,16,128]{2,1,0:T(8,128)(2,1)}), bf16[256,16,128]{2,1,0:T(8,128)(2,1)S(1)}, u32[]{:S(2)}, u32[]{:S(2)}) async-start(bf16[256,16,128]{2,1,0:T(8,128)(2,1)} %bitcast.3), calls=%async_computation.1 | async-start | bytes 2097152 | tf_op jit(solution)/shard_map/all_to_all | solution.py:242
  69.2 1.0 copy-start.3
  70.3 29.6 %copy-start = (bf16[2,128,512]{2,1,0:T(8,128)(2,1)S(1)}, bf16[2,128,512]{2,1,0:T(8,128)(2,1)}, u32[]{:S(2)}) copy-start(bf16[2,128,512]{2,1,0:T(8,128)(2,1)} %w_ref.3) | copy-start | bytes 786436
  70.3 29.6 %copy-start.4 = (bf16[2,128,128]{2,1,0:T(8,128)(2,1)S(1)}, bf16[2,128,128]{2,1,0:T(8,128)(2,1)}, u32[]{:S(2)}) copy-start(bf16[2,128,128]{2,1,0:T(8,128)(2,1)} %ow_ref.3) | copy-start | bytes 196612
  71.0 0.8 copy-start.1
  99.9 1.0 copy-start.2
  139.9 4.5 %collective-permute-start.1 = (bf16[8,16,2,16,128]{4,3,2,1,0:T(8,128)(2,1)S(1)}, bf16[8,16,2,16,128]{4,3,2,1,0:T(8,128)(2,1)S(1)}, u32[]{:S(2)}, u32[]{:S(2)}) collective-permute-start(bf16[8,16,2,16,128]{4,3,2,1,0:T(8,128)(2,1)S(1)} %bitcast.13), channel_id=1, source_target_pairs={{0,16},{16,0},{1,17},{17,1},{2,18},{18,2},{3,19},{19,3},{4,20},{20... | collective-permute-start | bytes 3145736 | tf_op jit(solution)/shard_map/ppermute | solution.py:247
  147.0 41.5 %all-to-all-start.3 = ((bf16[256,16,128]{2,1,0:T(8,128)(2,1)}), bf16[256,16,128]{2,1,0:T(8,128)(2,1)S(1)}, u32[]{:S(2)}, u32[]{:S(2)}) async-start(bf16[256,16,128]{2,1,0:T(8,128)(2,1)} %bitcast.7), calls=%async_computation.3 | async-start | bytes 2097152 | tf_op jit(solution)/shard_map/all_to_all | solution.py:242

commit v6 on v5

--- a/solution.py
+++ b/solution.py
@@ -242,14 +242,18 @@
     return lax.all_to_all(tiles, group, split_axis=0, concat_axis=0, tiled=True)
 
 
-def _products(kernel, group, sources, scratch, tiles):
-    own = _exchange(tiles.reshape(128, 32, 128), group).reshape(*sources, 2, 16, 128)
+def _operands(tiles, group, sources):
+    return _exchange(tiles.reshape(128, 32, 128), group).reshape(*sources, 2, 16, 128)
+
+
+def _products(kernel, scratch, own, gate):
     other = lax.ppermute(own, "core", [(0, 1), (1, 0)])
+    other, gate = lax.optimization_barrier((other, gate))
     core = lax.axis_index("core").astype(jnp.int32).reshape(1)
     (out,) = _call(
         kernel, [((16, 16, 16, 128), BF16)], scratch, (core, own, other), scalar=True
     )
-    return _exchange(out.reshape(256, 16, 128), ("zhi", "yhi", "ylo", "zlo", "xhi", "xlo"))
+    return _exchange(out.reshape(256, 16, 128), ("zhi", "yhi", "ylo", "zlo", "xhi", "xlo")), gate
 
 
 def body(pair_rep, in_gain, in_bias, proj_w, gate_w, out_gain, out_bias, out_w):
@@ -262,27 +266,28 @@
         [],
         (again, in_gain, in_bias, gate_w, out_gain, out_bias),
     )
-    tri = _products(
+    tri, gate = _products(
         _outgoing_kernel,
-        OUTGOING,
-        (16, 8),
         [((16, 2, 16, 512), BF16), ((16, 2, 2, 16, 512), BF16)],
-        tiles,
-    ).reshape(64, 2, 2, 16, 128)
+        _operands(tiles, OUTGOING, (16, 8)),
+        gate,
+    )
+    tri = tri.reshape(64, 2, 2, 16, 128)
     middle, tiles = _call(
         _middle_kernel,
         [(turned, BF16), ((4096, 128), BF16)],
         [PRODUCT_SCRATCH, OPERAND_SCRATCH],
         (tri, cells, gate, columns, out_w, proj_w),
     )
-    (gate,) = _call(_middle_gate_kernel, [(turned, F32)], [], (middle, columns, gate_w))
-    tri = _products(
+    own, again = lax.optimization_barrier((_operands(tiles, INCOMING, (8, 16)), middle))
+    (gate,) = _call(_middle_gate_kernel, [(turned, F32)], [], (again, columns, gate_w))
+    tri, gate = _products(
         _incoming_kernel,
-        INCOMING,
-        (8, 16),
         [((2, 2, 8, 16, 512), BF16), ((2, 2, 8, 16, 1024), BF16)],
-        tiles,
-    ).reshape(2, 2, 64, 16, 128)
+        own,
+        gate,
+    )
+    tri = tri.reshape(2, 2, 64, 16, 128)
     (out,) = _call(
         _last_kernel,
         [(pair_rep.shape, BF16)],

time: 193 us -> 189 us (0.979)
  blocking collectives: 86.1 us -> 168 us
  waiting for transfers between devices: 63.8 us -> 3.27 us
  starting transfers between devices: 24.6 us -> 3.82 us
  local copies, waits for them, and re-layouts: 2.9 us -> 0.66 us
    all_to_all x2 -> x4, blocking collectives: 86.1 us -> 168 us  [_exchange(): return lax.all_to_all(tiles, group, split_axis=0, concat_axis=0, tiled=True)]
    all_to_all x2 -> x0, waiting for transfers between devices: 58.6 us -> none  [_exchange(): return lax.all_to_all(tiles, group, split_axis=0, concat_axis=0, tiled=True)]
    all_to_all x2 -> x0, starting transfers between devices: 20.8 us -> none  [_exchange(): return lax.all_to_all(tiles, group, split_axis=0, concat_axis=0, tiled=True)]
    unnamed x20 -> x16, local copies, waits for them, and re-layouts: 2.9 us -> 0.66 us
    ppermute x2, waiting for transfers between devices: 5.25 us -> 3.27 us  [_products(): other = lax.ppermute(own, 'core', [(0, 1), (1, 0)])]
  transfers between devices with their start and end apart: 4 -> 2, of which waited for: 4 -> 2; matrix products, arithmetic and copies ran while one was open for 0% -> 0% of each run, Pallas kernels for 1% -> 1%
where the time goes in v6:
time: 189 us; the launch traced here: 187 us
  blocking collectives  168 us (89%)
  Pallas kernels  10.8 us (6%)
  starting transfers between devices  3.82 us (2%)
  waiting for transfers between devices  3.27 us (2%)
    all_to_all x4, blocking collectives, _exchange(): return lax.all_to_all(tiles, group, split_axis=0, concat_axis=0, tiled=True)  168 us
    pallas_call x6, Pallas kernels, _call(): pl.pallas_call(kernel, out_shape=[jax.ShapeDtypeStruct(shape, dtype) for...  7.58 us
    ppermute x2, starting transfers between devices, _products(): other = lax.ppermute(own, 'core', [(0, 1), (1, 0)])  3.82 us
  transfers between devices with their start and end apart: 2, of which 2 were waited for; matrix products, arithmetic and copies ran while one was open for 0% of the time, Pallas kernels for 1%

profile of v6, /device:TPU:6, one launch (start us, length us, event | category | flops | bytes accessed | tf_op | source)
XLA Modules:
  0.0 186.9 jit_solution(7211227015483250078)
XLA Ops:
  0.0 3.2 %shard_map.82 = bf16[4096,128]{1,0:T(8,128)(2,1)} custom-call(bf16[32,64,128]{2,1,0:T(8,128)(2,1)} %p_ref.2, f32[2,128]{1,0:T(2,128)} %gain_ref.3, f32[2,128]{1,0:T(2,128)} %bias_ref.3, bf16[2,128,512]{2,1,0:T(8,128)(2,1)} %w_ref.3), custom_call_target="tpu_custom_call" | custom-call | tf_op jit(solution)/shard_map/pallas_call | solution.py:230
  3.2 0.0 copy-start.1
  3.2 0.0 copy-start.3
  3.2 0.0 copy-start.5
  3.2 0.0 copy-start.6
  3.2 0.0 copy-start.7
  3.2 49.1 %all_to_all.20 = bf16[128,32,128]{2,1,0:T(8,128)(2,1)S(1)} all-to-all(bf16[128,32,128]{2,1,0:T(8,128)(2,1)} %bitcast.18), channel_id=1, replica_groups=mesh['zhi'=2,'yhi'=2,'ylo'=4,'core'=2,'zlo'=4,'xhi'=2,'xlo'=2] {'zhi','y..., dimensions={0} | all-to-all | bytes 2097152 | tf_op jit(solution)/shard_map/all_to_all | solution.py:242
  52.3 1.9 %collective-permute-start = (bf16[16,8,2,16,128]{4,3,2,1,0:T(8,128)(2,1)S(1)}, bf16[16,8,2,16,128]{4,3,2,1,0:T(8,128)(2,1)S(1)}, u32[]{:S(2)}, u32[]{:S(2)}) collective-permute-start(bf16[16,8,2,16,128]{4,3,2,1,0:T(8,128)(2,1)S(1)} %bitcast.11), channel_id=1, source_target_pairs={{0,16},{16,0},{1,17},{17,1},{2,18},{18,2},{3,19},{19,3},{4,20},{20... | collective-permute-start | bytes 3145736 | tf_op jit(solution)/shard_map/ppermute | solution.py:250
  54.2 0.0 copy-start.4
  54.2 0.0 copy-done.1
  54.3 0.0 copy-done.3
  54.3 0.0 copy-done.5
  54.3 0.0 copy-done.6
  54.3 0.0 copy-done.7
  54.3 0.6 copy-done.4
  54.9 0.7 shard_map.83
  55.6 1.2 collective-permute-done.other_ref
  56.9 1.2 shard_map.84
  58.0 0.0 copy-start
  58.0 0.0 copy-start.2
  58.1 40.8 %all_to_all.21 = bf16[256,16,128]{2,1,0:T(8,128)(2,1)S(1)} all-to-all(bf16[256,16,128]{2,1,0:T(8,128)(2,1)S(1)} %bitcast.16), channel_id=1, replica_groups=mesh['zhi'=2,'yhi'=2,'ylo'=4,'core'=2,'zlo'=4,'xhi'=2,'xlo'=2] {'zhi','y..., dimensions={0} | all-to-all | bytes 2097152 | tf_op jit(solution)/shard_map/all_to_all | solution.py:242
  98.8 0.0 copy-done
  98.8 0.0 copy-done.2
  98.9 1.9 shard_map.85
  100.7 37.2 %all_to_all.22 = bf16[128,32,128]{2,1,0:T(8,128)(2,1)S(1)} all-to-all(bf16[128,32,128]{2,1,0:T(8,128)(2,1)S(1)} %bitcast.17), channel_id=1, replica_groups=mesh['zhi'=2,'yhi'=2,'ylo'=4,'core'=2,'zlo'=4,'xhi'=2,'xlo'=2] {'zhi','y..., dimensions={0} | all-to-all | bytes 2097152 | tf_op jit(solution)/shard_map/all_to_all | solution.py:242
  137.9 1.9 %collective-permute-start.1 = (bf16[8,16,2,16,128]{4,3,2,1,0:T(8,128)(2,1)S(1)}, bf16[8,16,2,16,128]{4,3,2,1,0:T(8,128)(2,1)S(1)}, u32[]{:S(2)}, u32[]{:S(2)}) collective-permute-start(bf16[8,16,2,16,128]{4,3,2,1,0:T(8,128)(2,1)S(1)} %bitcast.13), channel_id=1, source_target_pairs={{0,16},{16,0},{1,17},{17,1},{2,18},{18,2},{3,19},{19,3},{4,20},{20... | collective-permute-start | bytes 3145736 | tf_op jit(solution)/shard_map/ppermute | solution.py:250
  139.8 0.6 shard_map.86.g_ref
  140.4 2.0 %collective-permute-done.1.other_ref = bf16[8,16,2,16,128]{4,3,2,1,0:T(8,128)(2,1)S(1)} collective-permute-done((bf16[8,16,2,16,128]{4,3,2,1,0:T(8,128)(2,1)S(1)}, bf16[8,16,2,16,128]{4,3,2,1,0:T(8,128)(2,1)S(1)}, u32[]{:S(2)}, u32[]{:S(2)}) %collective-permute-start.1) | collective-permute-done | bytes 1048608 | tf_op jit(solution)/shard_map/ppermute | solution.py:250
  142.4 1.6 shard_map.87
  144.0 41.2 %all_to_all.23 = bf16[256,16,128]{2,1,0:T(8,128)(2,1)S(1)} all-to-all(bf16[256,16,128]{2,1,0:T(8,128)(2,1)S(1)} %bitcast.15), channel_id=1, replica_groups=mesh['zhi'=2,'yhi'=2,'ylo'=4,'core'=2,'zlo'=4,'xhi'=2,'xlo'=2] {'zhi','y..., dimensions={0} | all-to-all | bytes 2097152 | tf_op jit(solution)/shard_map/all_to_all | solution.py:242
  185.2 1.7 shard_map.88
Async XLA Ops:
  3.2 51.1 %copy-start.1 = (bf16[32,64,128]{2,1,0:T(8,128)(2,1)S(1)}, bf16[32,64,128]{2,1,0:T(8,128)(2,1)}, u32[]{:S(2)}) copy-start(bf16[32,64,128]{2,1,0:T(8,128)(2,1)} %p_ref.2) | copy-start | bytes 1572868
  3.2 51.1 %copy-start.3 = (bf16[2,128,128]{2,1,0:T(8,128)(2,1)S(1)}, bf16[2,128,128]{2,1,0:T(8,128)(2,1)}, u32[]{:S(2)}) copy-start(bf16[2,128,128]{2,1,0:T(8,128)(2,1)} %gw_ref.3) | copy-start | bytes 196612
  3.2 51.1 %copy-start.5 = (f32[2,128]{1,0:T(2,128)S(1)}, f32[2,128]{1,0:T(2,128)}, u32[]{:S(2)}) copy-start(f32[2,128]{1,0:T(2,128)} %bias_ref.3) | copy-start | bytes 3076
  3.2 51.1 %copy-start.6 = (f32[2,128]{1,0:T(2,128)S(1)}, f32[2,128]{1,0:T(2,128)}, u32[]{:S(2)}) copy-start(f32[2,128]{1,0:T(2,128)} %og_ref.1) | copy-start | bytes 3076
  3.2 51.1 %copy-start.7 = (f32[2,128]{1,0:T(2,128)S(1)}, f32[2,128]{1,0:T(2,128)}, u32[]{:S(2)}) copy-start(f32[2,128]{1,0:T(2,128)} %ob_ref.1) | copy-start | bytes 3076
  52.3 4.5 %collective-permute-start = (bf16[16,8,2,16,128]{4,3,2,1,0:T(8,128)(2,1)S(1)}, bf16[16,8,2,16,128]{4,3,2,1,0:T(8,128)(2,1)S(1)}, u32[]{:S(2)}, u32[]{:S(2)}) collective-permute-start(bf16[16,8,2,16,128]{4,3,2,1,0:T(8,128)(2,1)S(1)} %bitcast.11), channel_id=1, source_target_pairs={{0,16},{16,0},{1,17},{17,1},{2,18},{18,2},{3,19},{19,3},{4,20},{20... | collective-permute-start | bytes 3145736 | tf_op jit(solution)/shard_map/ppermute | solution.py:250
  54.2 0.7 copy-start.4
  58.0 40.8 %copy-start = (bf16[2,128,512]{2,1,0:T(8,128)(2,1)S(1)}, bf16[2,128,512]{2,1,0:T(8,128)(2,1)}, u32[]{:S(2)}) copy-start(bf16[2,128,512]{2,1,0:T(8,128)(2,1)} %w_ref.3) | copy-start | bytes 786436
  58.0 40.8 %copy-start.2 = (bf16[2,128,128]{2,1,0:T(8,128)(2,1)S(1)}, bf16[2,128,128]{2,1,0:T(8,128)(2,1)}, u32[]{:S(2)}) copy-start(bf16[2,128,128]{2,1,0:T(8,128)(2,1)} %ow_ref.3) | copy-start | bytes 196612
  137.9 4.5 %collective-permute-start.1 = (bf16[8,16,2,16,128]{4,3,2,1,0:T(8,128)(2,1)S(1)}, bf16[8,16,2,16,128]{4,3,2,1,0:T(8,128)(2,1)S(1)}, u32[]{:S(2)}, u32[]{:S(2)}) collective-permute-start(bf16[8,16,2,16,128]{4,3,2,1,0:T(8,128)(2,1)S(1)} %bitcast.13), channel_id=1, source_target_pairs={{0,16},{16,0},{1,17},{17,1},{2,18},{18,2},{3,19},{19,3},{4,20},{20... | collective-permute-start | bytes 3145736 | tf_op jit(solution)/shard_map/ppermute | solution.py:250

commit v7 on v5

--- a/solution.py
+++ b/solution.py
@@ -181,27 +181,35 @@
         _put_products(out_ref, rows, tri)
 
 
-def _incoming_kernel(core_ref, own_ref, other_ref, out_ref, l_scr, r_scr):
+def _incoming_rows(core_ref, ref, l_ref, r_ref):
     def load_left(core):
-        for at, ref in ((0, own_ref), (1, other_ref)):
-            for zlo in range(4):
-                parts = [ref[:, zlo * 4 + x, 0] for x in range(4)]
-                lanes = slice(zlo * 128, zlo * 128 + 128)
-                for b in range(2):
-                    l_scr[at, b, :, :, lanes] = _quarter(parts, 2 * b + core)
+        for zlo in range(4):
+            parts = [ref[:, zlo * 4 + x, 0] for x in range(4)]
+            lanes = slice(zlo * 128, zlo * 128 + 128)
+            for b in range(2):
+                l_ref[b, :, :, lanes] = _quarter(parts, 2 * b + core)
 
     for core in range(2):
         pl.when(core_ref[0] == core)(functools.partial(load_left, core))
-    for at, ref in ((0, own_ref), (1, other_ref)):
-        for pair in range(8):
-            lanes = slice(pair * 128, pair * 128 + 128)
-            right = _pair_up(ref[:, 2 * pair, 1], ref[:, 2 * pair + 1, 1])
-            for b in range(2):
-                r_scr[at, b, :, :, lanes] = right[b]
-    right = r_scr[...].reshape(512, 1024)
+    for pair in range(8):
+        lanes = slice(pair * 128, pair * 128 + 128)
+        right = _pair_up(ref[:, 2 * pair, 1], ref[:, 2 * pair + 1, 1])
+        for b in range(2):
+            r_ref[b, :, :, lanes] = right[b]
+
+
+def _incoming_kernel(core_ref, other_ref, l_own, r_own, out_ref, l_scr, r_scr):
+    _incoming_rows(core_ref, other_ref, l_scr, r_scr)
+    rights = r_own[...].reshape(256, 1024), r_scr[...].reshape(256, 1024)
     for part in range(2):
-        left = l_scr[:, :, :, :, part * 256 : part * 256 + 256].reshape(512, 256)
-        tri = lax.dot_general(left, right, (((0,), (0,)), ((), ())), preferred_element_type=F32)
+        lanes = slice(part * 256, part * 256 + 256)
+        lefts = l_own[:, :, :, lanes].reshape(256, 256), l_scr[:, :, :, lanes].reshape(256, 256)
+        tri = lax.dot_general(
+            jnp.concatenate(lefts, axis=0),
+            jnp.concatenate(rights, axis=0),
+            (((0,), (0,)), ((), ())),
+            preferred_element_type=F32,
+        )
         _put_products(out_ref, slice(part * 8, part * 8 + 8), tri)
 
 
@@ -242,13 +250,21 @@
     return lax.all_to_all(tiles, group, split_axis=0, concat_axis=0, tiled=True)
 
 
-def _products(kernel, group, sources, scratch, tiles):
-    own = _exchange(tiles.reshape(128, 32, 128), group).reshape(*sources, 2, 16, 128)
+def _operands(tiles, group, sources):
+    return _exchange(tiles.reshape(128, 32, 128), group).reshape(*sources, 2, 16, 128)
+
+
+def _core():
+    return lax.axis_index("core").astype(jnp.int32).reshape(1)
+
+
+def _swap(own, *made):
     other = lax.ppermute(own, "core", [(0, 1), (1, 0)])
-    core = lax.axis_index("core").astype(jnp.int32).reshape(1)
-    (out,) = _call(
-        kernel, [((16, 16, 16, 128), BF16)], scratch, (core, own, other), scalar=True
-    )
+    return lax.optimization_barrier((other, *made))
+
+
+def _products(kernel, scratch, *args):
+    (out,) = _call(kernel, [((16, 16, 16, 128), BF16)], scratch, (_core(), *args), scalar=True)
     return _exchange(out.reshape(256, 16, 128), ("zhi", "yhi", "ylo", "zlo", "xhi", "xlo"))
 
 
@@ -262,12 +278,13 @@
         [],
         (again, in_gain, in_bias, gate_w, out_gain, out_bias),
     )
+    own = _operands(tiles, OUTGOING, (16, 8))
+    other, gate = _swap(own, gate)
     tri = _products(
         _outgoing_kernel,
-        OUTGOING,
-        (16, 8),
         [((16, 2, 16, 512), BF16), ((16, 2, 2, 16, 512), BF16)],
-        tiles,
+        own,
+        other,
     ).reshape(64, 2, 2, 16, 128)
     middle, tiles = _call(
         _middle_kernel,
@@ -275,14 +292,12 @@
         [PRODUCT_SCRATCH, OPERAND_SCRATCH],
         (tri, cells, gate, columns, out_w, proj_w),
     )
-    (gate,) = _call(_middle_gate_kernel, [(turned, F32)], [], (middle, columns, gate_w))
-    tri = _products(
-        _incoming_kernel,
-        INCOMING,
-        (8, 16),
-        [((2, 2, 8, 16, 512), BF16), ((2, 2, 8, 16, 1024), BF16)],
-        tiles,
-    ).reshape(2, 2, 64, 16, 128)
+    own, again = lax.optimization_barrier((_operands(tiles, INCOMING, (8, 16)), middle))
+    (gate,) = _call(_middle_gate_kernel, [(turned, F32)], [], (again, columns, gate_w))
+    rows = [((2, 8, 16, 512), BF16), ((2, 8, 16, 1024), BF16)]
+    left, right = _call(_incoming_rows, rows, [], (_core(), own), scalar=True)
+    other, gate, left, right = _swap(own, gate, left, right)
+    tri = _products(_incoming_kernel, rows, other, left, right).reshape(2, 2, 64, 16, 128)
     (out,) = _call(
         _last_kernel,
         [(pair_rep.shape, BF16)],

time: 193 us -> 189 us (0.979)
  blocking collectives: 86.1 us -> 168 us
  waiting for transfers between devices: 63.8 us -> 2.77 us
  starting transfers between devices: 24.6 us -> 3.82 us
  local copies, waits for them, and re-layouts: 2.9 us -> 0.66 us
    all_to_all x2 -> x4, blocking collectives: 86.1 us -> 168 us  [_exchange(): return lax.all_to_all(tiles, group, split_axis=0, concat_axis=0, tiled=True)]
    all_to_all x2 -> x0, waiting for transfers between devices: 58.6 us -> none  [_exchange(): return lax.all_to_all(tiles, group, split_axis=0, concat_axis=0, tiled=True)]
    all_to_all x2 -> x0, starting transfers between devices: 20.8 us -> none  [_exchange(): return lax.all_to_all(tiles, group, split_axis=0, concat_axis=0, tiled=True)]
    ppermute x2, waiting for transfers between devices: 5.25 us -> 2.77 us  [_swap(): other = lax.ppermute(own, 'core', [(0, 1), (1, 0)])]
    unnamed x20 -> x16, local copies, waits for them, and re-layouts: 2.9 us -> 0.66 us
    pallas_call x6 -> x7, Pallas kernels: 9.44 us -> 7.64 us  [_call(): pl.pallas_call(kernel, out_shape=[jax.ShapeDtypeStruct(shape, dtype) for...]
  transfers between devices with their start and end apart: 4 -> 2, of which waited for: 4 -> 2; matrix products, arithmetic and copies ran while one was open for 0% -> 0% of each run, Pallas kernels for 1% -> 1%
where the time goes in v7:
time: 189 us; the launch traced here: 186 us
  blocking collectives  168 us (89%)
  Pallas kernels  10.8 us (6%)
  starting transfers between devices  3.82 us (2%)
  waiting for transfers between devices  2.77 us (1%)
    all_to_all x4, blocking collectives, _exchange(): return lax.all_to_all(tiles, group, split_axis=0, concat_axis=0, tiled=True)  168 us
    pallas_call x7, Pallas kernels, _call(): pl.pallas_call(kernel, out_shape=[jax.ShapeDtypeStruct(shape, dtype) for...  7.64 us
    ppermute x2, starting transfers between devices, _swap(): other = lax.ppermute(own, 'core', [(0, 1), (1, 0)])  3.82 us
  transfers between devices with their start and end apart: 2, of which 2 were waited for; matrix products, arithmetic and copies ran while one was open for 0% of the time, Pallas kernels for 1%

profile of v7, /device:TPU:6, one launch (start us, length us, event | category | flops | bytes accessed | tf_op | source)
XLA Modules:
  0.0 186.5 jit_solution(3972026733830372800)
XLA Ops:
  0.0 3.2 %shard_map.82 = bf16[4096,128]{1,0:T(8,128)(2,1)} custom-call(bf16[32,64,128]{2,1,0:T(8,128)(2,1)} %p_ref.2, f32[2,128]{1,0:T(2,128)} %gain_ref.3, f32[2,128]{1,0:T(2,128)} %bias_ref.3, bf16[2,128,512]{2,1,0:T(8,128)(2,1)} %w_ref.3), custom_call_target="tpu_custom_call" | custom-call | tf_op jit(solution)/shard_map/pallas_call | solution.py:238
  3.2 0.0 copy-start.1
  3.2 0.0 copy-start.3
  3.2 0.0 copy-start.5
  3.2 0.0 copy-start.6
  3.2 0.0 copy-start.7
  3.2 49.1 %all_to_all.20 = bf16[128,32,128]{2,1,0:T(8,128)(2,1)S(1)} all-to-all(bf16[128,32,128]{2,1,0:T(8,128)(2,1)} %bitcast.18), channel_id=1, replica_groups=mesh['zhi'=2,'yhi'=2,'ylo'=4,'core'=2,'zlo'=4,'xhi'=2,'xlo'=2] {'zhi','y..., dimensions={0} | all-to-all | bytes 2097152 | tf_op jit(solution)/shard_map/all_to_all | solution.py:250
  52.3 1.9 %collective-permute-start = (bf16[16,8,2,16,128]{4,3,2,1,0:T(8,128)(2,1)S(1)}, bf16[16,8,2,16,128]{4,3,2,1,0:T(8,128)(2,1)S(1)}, u32[]{:S(2)}, u32[]{:S(2)}) collective-permute-start(bf16[16,8,2,16,128]{4,3,2,1,0:T(8,128)(2,1)S(1)} %bitcast.12), channel_id=1, source_target_pairs={{0,16},{16,0},{1,17},{17,1},{2,18},{18,2},{3,19},{19,3},{4,20},{20... | collective-permute-start | bytes 3145736 | tf_op jit(solution)/shard_map/ppermute | solution.py:262
  54.2 0.0 copy-start.4
  54.2 0.0 copy-done.1
  54.3 0.0 copy-done.3
  54.3 0.0 copy-done.5
  54.3 0.0 copy-done.6
  54.3 0.0 copy-done.7
  54.3 0.6 copy-done.4
  54.9 0.7 shard_map.83
  55.6 1.2 collective-permute-done.other_ref
  56.9 1.2 shard_map.84
  58.0 0.0 copy-start
  58.0 0.0 copy-start.2
  58.1 40.8 %all_to_all.21 = bf16[256,16,128]{2,1,0:T(8,128)(2,1)S(1)} all-to-all(bf16[256,16,128]{2,1,0:T(8,128)(2,1)S(1)} %bitcast.16), channel_id=1, replica_groups=mesh['zhi'=2,'yhi'=2,'ylo'=4,'core'=2,'zlo'=4,'xhi'=2,'xlo'=2] {'zhi','y..., dimensions={0} | all-to-all | bytes 2097152 | tf_op jit(solution)/shard_map/all_to_all | solution.py:250
  98.9 0.0 copy-done
  98.9 0.0 copy-done.2
  98.9 1.8 shard_map.85
  100.7 37.1 %all_to_all.22 = bf16[128,32,128]{2,1,0:T(8,128)(2,1)S(1)} all-to-all(bf16[128,32,128]{2,1,0:T(8,128)(2,1)S(1)} %bitcast.17), channel_id=1, replica_groups=mesh['zhi'=2,'yhi'=2,'ylo'=4,'core'=2,'zlo'=4,'xhi'=2,'xlo'=2] {'zhi','y..., dimensions={0} | all-to-all | bytes 2097152 | tf_op jit(solution)/shard_map/all_to_all | solution.py:250
  137.8 1.9 %collective-permute-start.1 = (bf16[8,16,2,16,128]{4,3,2,1,0:T(8,128)(2,1)S(1)}, bf16[8,16,2,16,128]{4,3,2,1,0:T(8,128)(2,1)S(1)}, u32[]{:S(2)}, u32[]{:S(2)}) collective-permute-start(bf16[8,16,2,16,128]{4,3,2,1,0:T(8,128)(2,1)S(1)} %bitcast.14), channel_id=1, source_target_pairs={{0,16},{16,0},{1,17},{17,1},{2,18},{18,2},{3,19},{19,3},{4,20},{20... | collective-permute-start | bytes 3145736 | tf_op jit(solution)/shard_map/ppermute | solution.py:262
  139.7 0.5 shard_map.87
  140.2 0.6 shard_map.86.g_ref
  140.8 1.5 collective-permute-done.1.other_ref
  142.4 1.2 shard_map.88
  143.6 41.2 %all_to_all.23 = bf16[256,16,128]{2,1,0:T(8,128)(2,1)S(1)} all-to-all(bf16[256,16,128]{2,1,0:T(8,128)(2,1)S(1)} %bitcast.10), channel_id=1, replica_groups=mesh['zhi'=2,'yhi'=2,'ylo'=4,'core'=2,'zlo'=4,'xhi'=2,'xlo'=2] {'zhi','y..., dimensions={0} | all-to-all | bytes 2097152 | tf_op jit(solution)/shard_map/all_to_all | solution.py:250
  184.8 1.7 shard_map.89
Async XLA Ops:
  3.2 51.1 %copy-start.1 = (bf16[32,64,128]{2,1,0:T(8,128)(2,1)S(1)}, bf16[32,64,128]{2,1,0:T(8,128)(2,1)}, u32[]{:S(2)}) copy-start(bf16[32,64,128]{2,1,0:T(8,128)(2,1)} %p_ref.2) | copy-start | bytes 1572868
  3.2 51.1 %copy-start.3 = (bf16[2,128,128]{2,1,0:T(8,128)(2,1)S(1)}, bf16[2,128,128]{2,1,0:T(8,128)(2,1)}, u32[]{:S(2)}) copy-start(bf16[2,128,128]{2,1,0:T(8,128)(2,1)} %gw_ref.3) | copy-start | bytes 196612
  3.2 51.1 %copy-start.5 = (f32[2,128]{1,0:T(2,128)S(1)}, f32[2,128]{1,0:T(2,128)}, u32[]{:S(2)}) copy-start(f32[2,128]{1,0:T(2,128)} %bias_ref.3) | copy-start | bytes 3076
  3.2 51.1 %copy-start.6 = (f32[2,128]{1,0:T(2,128)S(1)}, f32[2,128]{1,0:T(2,128)}, u32[]{:S(2)}) copy-start(f32[2,128]{1,0:T(2,128)} %og_ref.1) | copy-start | bytes 3076
  3.2 51.1 %copy-start.7 = (f32[2,128]{1,0:T(2,128)S(1)}, f32[2,128]{1,0:T(2,128)}, u32[]{:S(2)}) copy-start(f32[2,128]{1,0:T(2,128)} %ob_ref.1) | copy-start | bytes 3076
  52.3 4.5 %collective-permute-start = (bf16[16,8,2,16,128]{4,3,2,1,0:T(8,128)(2,1)S(1)}, bf16[16,8,2,16,128]{4,3,2,1,0:T(8,128)(2,1)S(1)}, u32[]{:S(2)}, u32[]{:S(2)}) collective-permute-start(bf16[16,8,2,16,128]{4,3,2,1,0:T(8,128)(2,1)S(1)} %bitcast.12), channel_id=1, source_target_pairs={{0,16},{16,0},{1,17},{17,1},{2,18},{18,2},{3,19},{19,3},{4,20},{20... | collective-permute-start | bytes 3145736 | tf_op jit(solution)/shard_map/ppermute | solution.py:262
  54.2 0.7 copy-start.4
  58.0 40.8 %copy-start = (bf16[2,128,512]{2,1,0:T(8,128)(2,1)S(1)}, bf16[2,128,512]{2,1,0:T(8,128)(2,1)}, u32[]{:S(2)}) copy-start(bf16[2,128,512]{2,1,0:T(8,128)(2,1)} %w_ref.3) | copy-start | bytes 786436
  58.0 40.8 %copy-start.2 = (bf16[2,128,128]{2,1,0:T(8,128)(2,1)S(1)}, bf16[2,128,128]{2,1,0:T(8,128)(2,1)}, u32[]{:S(2)}) copy-start(bf16[2,128,128]{2,1,0:T(8,128)(2,1)} %ow_ref.3) | copy-start | bytes 196612
  137.8 4.5 %collective-permute-start.1 = (bf16[8,16,2,16,128]{4,3,2,1,0:T(8,128)(2,1)S(1)}, bf16[8,16,2,16,128]{4,3,2,1,0:T(8,128)(2,1)S(1)}, u32[]{:S(2)}, u32[]{:S(2)}) collective-permute-start(bf16[8,16,2,16,128]{4,3,2,1,0:T(8,128)(2,1)S(1)} %bitcast.14), channel_id=1, source_target_pairs={{0,16},{16,0},{1,17},{17,1},{2,18},{18,2},{3,19},{19,3},{4,20},{20... | collective-permute-start | bytes 3145736 | tf_op jit(solution)/shard_map/ppermute | solution.py:262

commit v8 on v7

--- a/solution.py
+++ b/solution.py
@@ -174,11 +174,9 @@
             r_scr[:, pl.ds(core, 1), b, :, lanes] = right[b][:, None]
             r_scr[:, pl.ds(1 - core, 1), b, :, lanes] = away[b][:, None]
     right = r_scr[...].reshape(1024, 512)
-    for part in range(2):
-        rows = slice(part * 8, part * 8 + 8)
-        left = l_scr[rows].reshape(256, 512)
-        tri = lax.dot_general(left, right, (((1,), (1,)), ((), ())), preferred_element_type=F32)
-        _put_products(out_ref, rows, tri)
+    left = l_scr[...].reshape(512, 512)
+    tri = lax.dot_general(left, right, (((1,), (1,)), ((), ())), preferred_element_type=F32)
+    _put_products(out_ref, slice(0, 16), tri)
 
 
 def _incoming_rows(core_ref, ref, l_ref, r_ref):

time: 189 us -> 189 us (level)
  no operation moved by 1% of the time
where the time goes in v8:
time: 189 us; the launch traced here: 186 us
  blocking collectives  168 us (89%)
  Pallas kernels  10.8 us (6%)
  starting transfers between devices  3.82 us (2%)
  waiting for transfers between devices  2.77 us (1%)
    all_to_all x4, blocking collectives, _exchange(): return lax.all_to_all(tiles, group, split_axis=0, concat_axis=0, tiled=True)  168 us
    pallas_call x7, Pallas kernels, _call(): pl.pallas_call(kernel, out_shape=[jax.ShapeDtypeStruct(shape, dtype) for...  7.63 us
    ppermute x2, starting transfers between devices, _swap(): other = lax.ppermute(own, 'core', [(0, 1), (1, 0)])  3.82 us
  transfers between devices with their start and end apart: 2, of which 2 were waited for; matrix products, arithmetic and copies ran while one was open for 0% of the time, Pallas kernels for 1%

profile of v8, /device:TPU:6, one launch (start us, length us, event | category | flops | bytes accessed | tf_op | source)
XLA Modules:
  0.0 186.5 jit_solution(17481407975950579909)
XLA Ops:
  0.0 3.2 %shard_map.82 = bf16[4096,128]{1,0:T(8,128)(2,1)} custom-call(bf16[32,64,128]{2,1,0:T(8,128)(2,1)} %p_ref.2, f32[2,128]{1,0:T(2,128)} %gain_ref.3, f32[2,128]{1,0:T(2,128)} %bias_ref.3, bf16[2,128,512]{2,1,0:T(8,128)(2,1)} %w_ref.3), custom_call_target="tpu_custom_call" | custom-call | tf_op jit(solution)/shard_map/pallas_call | solution.py:236
  3.2 0.0 copy-start.1
  3.2 0.0 copy-start.3
  3.2 0.0 copy-start.5
  3.2 0.0 copy-start.6
  3.2 0.0 copy-start.7
  3.2 49.1 %all_to_all.20 = bf16[128,32,128]{2,1,0:T(8,128)(2,1)S(1)} all-to-all(bf16[128,32,128]{2,1,0:T(8,128)(2,1)} %bitcast.18), channel_id=1, replica_groups=mesh['zhi'=2,'yhi'=2,'ylo'=4,'core'=2,'zlo'=4,'xhi'=2,'xlo'=2] {'zhi','y..., dimensions={0} | all-to-all | bytes 2097152 | tf_op jit(solution)/shard_map/all_to_all | solution.py:248
  52.3 1.9 %collective-permute-start = (bf16[16,8,2,16,128]{4,3,2,1,0:T(8,128)(2,1)S(1)}, bf16[16,8,2,16,128]{4,3,2,1,0:T(8,128)(2,1)S(1)}, u32[]{:S(2)}, u32[]{:S(2)}) collective-permute-start(bf16[16,8,2,16,128]{4,3,2,1,0:T(8,128)(2,1)S(1)} %bitcast.12), channel_id=1, source_target_pairs={{0,16},{16,0},{1,17},{17,1},{2,18},{18,2},{3,19},{19,3},{4,20},{20... | collective-permute-start | bytes 3145736 | tf_op jit(solution)/shard_map/ppermute | solution.py:260
  54.2 0.0 copy-start.4
  54.2 0.0 copy-done.1
  54.3 0.0 copy-done.3
  54.3 0.0 copy-done.5
  54.3 0.0 copy-done.6
  54.3 0.0 copy-done.7
  54.3 0.6 copy-done.4
  54.9 0.7 shard_map.83
  55.6 1.2 collective-permute-done.other_ref
  56.9 1.2 shard_map.84
  58.0 0.0 copy-start
  58.0 0.0 copy-start.2
  58.1 40.8 %all_to_all.21 = bf16[256,16,128]{2,1,0:T(8,128)(2,1)S(1)} all-to-all(bf16[256,16,128]{2,1,0:T(8,128)(2,1)S(1)} %bitcast.16), channel_id=1, replica_groups=mesh['zhi'=2,'yhi'=2,'ylo'=4,'core'=2,'zlo'=4,'xhi'=2,'xlo'=2] {'zhi','y..., dimensions={0} | all-to-all | bytes 2097152 | tf_op jit(solution)/shard_map/all_to_all | solution.py:248
  98.9 0.0 copy-done
  98.9 0.0 copy-done.2
  98.9 1.8 shard_map.85
  100.7 37.2 %all_to_all.22 = bf16[128,32,128]{2,1,0:T(8,128)(2,1)S(1)} all-to-all(bf16[128,32,128]{2,1,0:T(8,128)(2,1)S(1)} %bitcast.17), channel_id=1, replica_groups=mesh['zhi'=2,'yhi'=2,'ylo'=4,'core'=2,'zlo'=4,'xhi'=2,'xlo'=2] {'zhi','y..., dimensions={0} | all-to-all | bytes 2097152 | tf_op jit(solution)/shard_map/all_to_all | solution.py:248
  137.8 1.9 %collective-permute-start.1 = (bf16[8,16,2,16,128]{4,3,2,1,0:T(8,128)(2,1)S(1)}, bf16[8,16,2,16,128]{4,3,2,1,0:T(8,128)(2,1)S(1)}, u32[]{:S(2)}, u32[]{:S(2)}) collective-permute-start(bf16[8,16,2,16,128]{4,3,2,1,0:T(8,128)(2,1)S(1)} %bitcast.14), channel_id=1, source_target_pairs={{0,16},{16,0},{1,17},{17,1},{2,18},{18,2},{3,19},{19,3},{4,20},{20... | collective-permute-start | bytes 3145736 | tf_op jit(solution)/shard_map/ppermute | solution.py:260
  139.7 0.5 shard_map.87
  140.2 0.6 shard_map.86.g_ref
  140.8 1.5 collective-permute-done.1.other_ref
  142.4 1.2 shard_map.88
  143.6 41.2 %all_to_all.23 = bf16[256,16,128]{2,1,0:T(8,128)(2,1)S(1)} all-to-all(bf16[256,16,128]{2,1,0:T(8,128)(2,1)S(1)} %bitcast.10), channel_id=1, replica_groups=mesh['zhi'=2,'yhi'=2,'ylo'=4,'core'=2,'zlo'=4,'xhi'=2,'xlo'=2] {'zhi','y..., dimensions={0} | all-to-all | bytes 2097152 | tf_op jit(solution)/shard_map/all_to_all | solution.py:248
  184.8 1.7 shard_map.89
Async XLA Ops:
  3.2 51.1 %copy-start.1 = (bf16[32,64,128]{2,1,0:T(8,128)(2,1)S(1)}, bf16[32,64,128]{2,1,0:T(8,128)(2,1)}, u32[]{:S(2)}) copy-start(bf16[32,64,128]{2,1,0:T(8,128)(2,1)} %p_ref.2) | copy-start | bytes 1572868
  3.2 51.1 %copy-start.3 = (bf16[2,128,128]{2,1,0:T(8,128)(2,1)S(1)}, bf16[2,128,128]{2,1,0:T(8,128)(2,1)}, u32[]{:S(2)}) copy-start(bf16[2,128,128]{2,1,0:T(8,128)(2,1)} %gw_ref.3) | copy-start | bytes 196612
  3.2 51.1 %copy-start.5 = (f32[2,128]{1,0:T(2,128)S(1)}, f32[2,128]{1,0:T(2,128)}, u32[]{:S(2)}) copy-start(f32[2,128]{1,0:T(2,128)} %bias_ref.3) | copy-start | bytes 3076
  3.2 51.1 %copy-start.6 = (f32[2,128]{1,0:T(2,128)S(1)}, f32[2,128]{1,0:T(2,128)}, u32[]{:S(2)}) copy-start(f32[2,128]{1,0:T(2,128)} %og_ref.1) | copy-start | bytes 3076
  3.2 51.1 %copy-start.7 = (f32[2,128]{1,0:T(2,128)S(1)}, f32[2,128]{1,0:T(2,128)}, u32[]{:S(2)}) copy-start(f32[2,128]{1,0:T(2,128)} %ob_ref.1) | copy-start | bytes 3076
  52.3 4.5 %collective-permute-start = (bf16[16,8,2,16,128]{4,3,2,1,0:T(8,128)(2,1)S(1)}, bf16[16,8,2,16,128]{4,3,2,1,0:T(8,128)(2,1)S(1)}, u32[]{:S(2)}, u32[]{:S(2)}) collective-permute-start(bf16[16,8,2,16,128]{4,3,2,1,0:T(8,128)(2,1)S(1)} %bitcast.12), channel_id=1, source_target_pairs={{0,16},{16,0},{1,17},{17,1},{2,18},{18,2},{3,19},{19,3},{4,20},{20... | collective-permute-start | bytes 3145736 | tf_op jit(solution)/shard_map/ppermute | solution.py:260
  54.2 0.7 copy-start.4
  58.0 40.8 %copy-start = (bf16[2,128,512]{2,1,0:T(8,128)(2,1)S(1)}, bf16[2,128,512]{2,1,0:T(8,128)(2,1)}, u32[]{:S(2)}) copy-start(bf16[2,128,512]{2,1,0:T(8,128)(2,1)} %w_ref.3) | copy-start | bytes 786436
  58.0 40.8 %copy-start.2 = (bf16[2,128,128]{2,1,0:T(8,128)(2,1)S(1)}, bf16[2,128,128]{2,1,0:T(8,128)(2,1)}, u32[]{:S(2)}) copy-start(bf16[2,128,128]{2,1,0:T(8,128)(2,1)} %ow_ref.3) | copy-start | bytes 196612
  137.8 4.5 %collective-permute-start.1 = (bf16[8,16,2,16,128]{4,3,2,1,0:T(8,128)(2,1)S(1)}, bf16[8,16,2,16,128]{4,3,2,1,0:T(8,128)(2,1)S(1)}, u32[]{:S(2)}, u32[]{:S(2)}) collective-permute-start(bf16[8,16,2,16,128]{4,3,2,1,0:T(8,128)(2,1)S(1)} %bitcast.14), channel_id=1, source_target_pairs={{0,16},{16,0},{1,17},{17,1},{2,18},{18,2},{3,19},{19,3},{4,20},{20... | collective-permute-start | bytes 3145736 | tf_op jit(solution)/shard_map/ppermute | solution.py:260
